TPU v7x, 128 devices: a whole 4x4x4 slice. The times are simulated.
128 devices in a mesh: gas: 64 (over y, x, z), grp: 2 (over core).
Axes of the slice: x: 4, y: 4, z: 4, core: 2. Of those that a mesh axis runs over, the one named last changes fastest.
Arguments:
- gas_state: float32 [6, 256, 64, 256], P(None, 'gas', 'grp')
- particle_blocks: float32 [5, 131072, 128], P(None, ('gas', 'grp'))
- owner: int32 [131072, 1], P(('gas', 'grp')), may hold values from 0 to 127; in each aligned block of 1024 rows (0 to 1023, 1024 to 2047, ...) at most 16 rows name the same one
- host_cell: int32 [131072], P(('gas', 'grp')), may hold values from 0 to 32767
- live_count: int32 [131072], P(('gas', 'grp')), may hold values from 1 to 128, as said below
Outputs:
- gas_next: float32 [6, 256, 64, 256], P(None, 'gas', 'grp')
- parcels_next: float32 [5, 131072, 128], P(None, ('gas', 'grp'))
Inputs may be any that keep to these rules, and one draw needn't show every extreme that they name: Among the blocks of one device, at most 16 name the same owner. `live_count`: the first block of every device is full.
All inputs are finite; a program needn't handle non-finite values.
Results may differ from a plain program's by a relative error of at most 0.00002.
Values sent between devices are 32-bit elements; how exact they have to be, the bound alone decides.
No kernel may reach another device: no remote copies, remote signals or barrier semaphores. Data moves between devices by JAX's collectives and lax.ppermute only.
A program may use at most 128 MiB of HBM per device.

v0:
```python
import jax
import jax.numpy as jnp
from jax import lax
from jax.experimental import pallas as pl
from jax.experimental.pallas import tpu as pltpu
from jax.sharding import PartitionSpec as P

AXES = ("gas", "grp")
DEVICES = 128
LANES = 128
CAP = 16
CX, CY, NZ = 4, 32, 256
ROWS = CX * CY
BLK_DEV = 1024
CHUNKS = BLK_DEV // LANES
NSUB = 4
NVAR = 5
PIECES = 3
HALO = 3
EXT_X = CX + 2 * HALO
EXT_Y = CY + 8

LAM = 0.1
GAMMA_ADIABATIC = 1.4
CLOCK_INCREMENT = 0.25
TAU_DRAG = 0.8
THERMAL_RELAX = 1.2
EVAP_RATE = 0.5
LATENT_EVAPORATE = 0.3
WEIGHT = 0.05
LOG2E = 1.4426950408889634

F32 = jnp.float32
BF16 = jnp.bfloat16
VMEM_LIMIT = 48 * 1024 * 1024


def iota(shape, dim):
    return lax.broadcasted_iota(jnp.int32, shape, dim)


def dot(a, b):
    return lax.dot_general(a, b, (((1,), (0,)), ((), ())), preferred_element_type=F32)


def dot_nt(a, b):
    return lax.dot_general(a, b, (((1,), (1,)), ((), ())), preferred_element_type=F32)


def split(x):
    pieces = []
    for _ in range(PIECES):
        piece = x.astype(BF16)
        pieces.append(piece)
        x = x - piece.astype(F32)
    return pieces


def ones_where(mask):
    return jnp.where(mask, 1.0, 0.0).astype(BF16)


def compiler_params():
    return pltpu.CompilerParams(vmem_limit_bytes=VMEM_LIMIT)


def request_kernel(owner_ref, cell_ref, req_ref, rank_ref):
    down = iota((LANES, LANES), 0)
    across = iota((LANES, LANES), 1)
    earlier = ones_where(down < across)
    every = jnp.ones((LANES, LANES), BF16)
    before = jnp.zeros((LANES, LANES), F32)
    total = jnp.zeros((LANES, LANES), F32)
    for i in range(CHUNKS):
        named = down == owner_ref[i : i + 1, :]
        hot = ones_where(named)
        count = dot(hot, earlier) + before
        rank = jnp.sum(jnp.where(named, count, 0.0), axis=0, keepdims=True).astype(jnp.int32)
        rank_ref[i : i + 1, :] = rank
        cell = cell_ref[i : i + 1, :]
        high = (((cell >> 8) + 1) << 8).astype(F32)
        low = (cell & 255).astype(F32)
        placed = down == rank
        total = total + dot_nt(hot, jnp.where(placed, high, 0.0).astype(BF16))
        total = total + dot_nt(hot, jnp.where(placed, low, 0.0).astype(BF16))
        before = before + dot(hot, every)
    req_ref[...] = total.astype(jnp.int32) - 256


def table_kernel(gas_ref, table_ref):
    inverse = 1.0 / gas_ref[0]
    for c in range(NVAR):
        value = gas_ref[1 + c] * inverse
        for half in range(2):
            turned = value[:, half * LANES : (half + 1) * LANES].T
            for p, piece in enumerate(split(turned)):
                start = p * 2 * ROWS + half * ROWS
                table_ref[c * LANES : (c + 1) * LANES, start : start + ROWS] = piece


def cell_parts(asked_ref):
    cell = asked_ref[...].astype(F32).T.astype(jnp.int32)
    return (cell >> 8) + ROWS * ((cell >> 7) & 1), cell & (LANES - 1)


def gather_kernel(asked_ref, table_ref, reply_ref, found):
    row, lane = cell_parts(asked_ref)
    table = table_ref[...]
    found[...] = jnp.zeros((LANES, LANES), F32)
    for pair in range(CAP // 2):
        k = 2 * pair
        rows = jnp.concatenate([row[k : k + 1], row[k + 1 : k + 2]], axis=1)
        lanes = jnp.concatenate([lane[k : k + 1], lane[k + 1 : k + 2]], axis=1)
        hot = ones_where(iota((2 * ROWS, 2 * LANES), 0) == rows)
        values = dot(table, jnp.concatenate([hot] * PIECES, axis=0))
        here = iota((LANES, 2 * LANES), 0) == lanes
        for c in range(NVAR):
            part = values[c * LANES : (c + 1) * LANES]
            picked = jnp.sum(jnp.where(here, part, 0.0), axis=0, keepdims=True)
            found[c * CAP + k : c * CAP + k + 1, :] = picked[:, :LANES]
            found[c * CAP + k + 1 : c * CAP + k + 2, :] = picked[:, LANES:]
    reply_ref[...] = found[...].T


def integrate(parcels, gas_vars):
    mass, speeds, thermal = parcels[0], parcels[1:4], parcels[4]
    ambient, vapor = gas_vars[3], gas_vars[4]
    level = jnp.log2(mass)
    gain = jnp.zeros_like(mass)
    exposure = jnp.zeros_like(mass)
    headroom = 0.3 - vapor
    for _ in range(NSUB):
        inverse = jnp.exp2((-2.0 / 3.0) * (level + gain))
        share = headroom - 0.3 * (1.0 / (1.0 + thermal * thermal))
        loss = (CLOCK_INCREMENT * EVAP_RATE * LOG2E) * share * inverse
        kept = jnp.exp2((-CLOCK_INCREMENT / THERMAL_RELAX * LOG2E) * inverse)
        thermal = (
            ambient
            + (thermal - ambient) * kept
            - LATENT_EVAPORATE * (jnp.exp2(loss) - 1.0)
        )
        gain = gain - loss
        exposure = exposure + inverse
    drag = jnp.exp2((-CLOCK_INCREMENT / TAU_DRAG * LOG2E) * exposure)
    moved = [gas_vars[c] + (speeds[c] - gas_vars[c]) * drag for c in range(3)]
    return [mass * jnp.exp2(gain)] + moved + [thermal]


def parcel_kernel(
    owner_ref, rank_ref, live_ref, ans_ref, old_ref, new_ref, send_ref, columns, answers, spread, gather
):
    step = pl.program_id(0)
    per_step = old_ref.shape[1] // LANES

    @pl.when(step == 0)
    def _():
        pad = jnp.zeros((LANES - 3 * CHUNKS, LANES), F32)
        rows = [owner_ref[...], rank_ref[...], live_ref[...]]
        stack = jnp.concatenate([r.astype(F32) for r in rows] + [pad], axis=0)
        columns[...] = stack.T.astype(BF16)
        answers[...] = jnp.concatenate(split(ans_ref[...]), axis=1)
        shape = (PIECES * LANES, NVAR * LANES)
        spread[...] = ones_where((iota(shape, 0) % LANES) // CAP == iota(shape, 1) // LANES)
        shape = (NVAR * LANES, LANES)
        gather[...] = ones_where(iota(shape, 0) // LANES == iota(shape, 1) // CAP)
        send_ref[...] = jnp.zeros((LANES, LANES), F32)

    across = iota((LANES, LANES), 1)
    for j in range(per_step):
        i = step * per_step + j
        shape = (LANES, 3 * LANES)
        chosen = ones_where(iota(shape, 0) == i + CHUNKS * (iota(shape, 1) // LANES))
        wide = dot(columns[...], chosen).astype(jnp.int32)
        owner, rank, live = (wide[:, s * LANES : (s + 1) * LANES] for s in range(3))
        slot = across % CAP == rank
        received = dot(ones_where(owner == across), answers[...])
        mine = jnp.where(jnp.concatenate([slot] * PIECES, axis=1), received, 0.0).astype(BF16)
        gas_wide = dot(mine, spread[...])
        gas_vars = [gas_wide[:, c * LANES : (c + 1) * LANES] for c in range(NVAR)]
        here = slice(j * LANES, (j + 1) * LANES)
        old = [old_ref[c, here, :] for c in range(5)]
        alive = across < live
        new = [jnp.where(alive, n, o) for n, o in zip(integrate(old, gas_vars), old)]
        for c in range(5):
            new_ref[c, here, :] = new[c]
        change = [new[0] - old[0]] + [new[0] * new[c] - old[0] * old[c] for c in range(1, 5)]
        pieces = split(jnp.concatenate(change, axis=1))
        summed = sum(dot(piece, gather[...]) for piece in pieces)
        placed = jnp.where(slot, -summed, 0.0)
        hot = ones_where(iota((LANES, LANES), 0) == owner_ref[pl.ds(i, 1), :])
        send_ref[...] += sum(dot(hot, piece) for piece in split(placed))


def scatter_kernel(asked_ref, come_ref, section_ref, out_ref, total):
    row, lane = cell_parts(asked_ref)
    pieces = [p.astype(F32) for p in split(come_ref[...].T)]
    for pair in range(CAP // 2):
        hots, parts = [], []
        for k in (2 * pair, 2 * pair + 1):
            hot = ones_where(iota((2 * ROWS, LANES), 0) == row[k : k + 1])
            here = iota((LANES, LANES), 0) == lane[k : k + 1]
            for piece in pieces:
                hots.append(hot)
                parts.append(
                    jnp.concatenate(
                        [
                            jnp.where(here, piece[c * CAP + k : c * CAP + k + 1], 0.0)
                            for c in range(NVAR)
                        ],
                        axis=0,
                    ).astype(BF16)
                )
        added = dot_nt(jnp.concatenate(parts, axis=1), jnp.concatenate(hots, axis=1))
        if pair == 0:
            total[...] = added
        else:
            total[...] += added
    for c in range(NVAR):
        for half in range(2):
            cells = WEIGHT * total[c * LANES : (c + 1) * LANES, half * ROWS : (half + 1) * ROWS].T
            z = slice(half * LANES, (half + 1) * LANES)
            out_ref[c, :, z] = section_ref[c, :, z] + cells
            if c == 0:
                out_ref[NVAR, :, z] = section_ref[NVAR, :, z] + cells


def gas_kernel(
    place_ref, gas_ref, edge_ref, low_ref, high_ref, out_ref, q0, q1, q2, prim, face
):
    pair, first, last = place_ref[0], place_ref[1], place_ref[2]
    own = pl.ds(pl.multiple_of(pair * 8, 8), CY)
    side = pl.ds(pl.multiple_of((1 - pair) * CY, 8), 8)
    inner = slice(HALO, HALO + CX)
    q0[:, inner, own, :] = gas_ref[...]
    q0[:, inner, side, :] = edge_ref[...]
    for ref, start in ((low_ref, 0), (high_ref, HALO + CX)):
        q0[:, start : start + HALO, own, :] = ref[:, :, :CY, :]
        q0[:, start : start + HALO, side, :] = ref[:, :, CY:, :]

    def ghosts(q):
        @pl.when(first == 1)
        def _():
            q[:, HALO - 1] = q[:, HALO]

        @pl.when(last == 1)
        def _():
            q[:, HALO + CX] = q[:, HALO + CX - 1]

    shape = (EXT_Y, NZ)
    ends = {
        0: (iota(shape, 0) == 0, iota(shape, 0) == EXT_Y - 1),
        1: (iota(shape, 1) == 0, iota(shape, 1) == NZ - 1),
    }

    def primitives(q, x):
        inverse = 1.0 / q[0, x]
        for d in range(3):
            prim[d, x] = q[1 + d, x] * inverse
        prim[3, x] = jnp.sqrt(GAMMA_ADIABATIC * (q[4, x] * inverse))

    def flux(values, speed, d, c, pressure):
        product = values * speed
        return product + pressure if c == 1 + d else product

    def x_faces(q, x):
        u, un = prim[0, x], prim[0, x + 1]
        rate = jnp.maximum(jnp.abs(u) + prim[3, x], jnp.abs(un) + prim[3, x + 1])
        faces = []
        for c in range(6):
            v, vn = q[c, x], q[c, x + 1]
            f = flux(v, u, 0, c, q[4, x])
            fn = flux(vn, un, 0, c, q[4, x + 1])
            faces.append(f + fn - rate * (vn - v))
        return faces

    def update(q, combine, start, stop):
        def fill(x, carry):
            primitives(q, x)
            return carry

        lax.fori_loop(start - 1, stop + 1, fill, 0)
        for c, value in enumerate(x_faces(q, start - 1)):
            face[c] = value

        def row(x, carry):
            upper = x_faces(q, x)
            change = []
            for c in range(6):
                change.append(upper[c] - face[c])
                face[c] = upper[c]
            for axis in (0, 1):
                d = 1 + axis
                size = shape[axis]
                lower_end, upper_end = ends[axis]
                u = prim[d, x]
                a = jnp.abs(u) + prim[3, x]
                un = pltpu.roll(u, size - 1, axis)
                rate = jnp.maximum(a, pltpu.roll(a, size - 1, axis))
                p = q[4, x]
                pn = pltpu.roll(p, size - 1, axis)
                for c in range(6):
                    v = q[c, x]
                    vn = pn if c == 4 else pltpu.roll(v, size - 1, axis)
                    f = flux(v, u, d, c, p)
                    g = f + flux(vn, un, d, c, pn) - rate * (vn - v)
                    twice = f + f
                    g = jnp.where(upper_end, twice, g)
                    below = jnp.where(lower_end, twice, pltpu.roll(g, 1, axis))
                    change[c] = change[c] + (g - below)
            for c in range(6):
                combine(c, x, q[c, x] - (0.5 * LAM) * change[c])
            return carry

        lax.fori_loop(start, stop, row, 0)

    ghosts(q0)

    def first_section(c, x, value):
        q1[c, x] = value

    update(q0, first_section, 1, EXT_X - 1)
    ghosts(q1)

    def second_section(c, x, value):
        q2[c, x] = 0.75 * q0[c, x] + 0.25 * value

    update(q1, second_section, 2, EXT_X - 2)
    ghosts(q2)

    def third_section(c, x, value):
        q1[c, x] = q0[c, x] * (1.0 / 3.0) + (2.0 / 3.0) * value

    update(q2, third_section, HALO, HALO + CX)
    out_ref[...] = q1[:, inner, own, :]


def whole(shape):
    return pl.BlockSpec(shape, lambda *_: (0,) * len(shape))


def call(kernel, outs, scratch=(), **more):
    return pl.pallas_call(
        kernel,
        out_shape=outs,
        scratch_shapes=list(scratch),
        compiler_params=compiler_params(),
        **more,
    )


def deliver(buffer):
    return lax.all_to_all(buffer, AXES, split_axis=0, concat_axis=0, tiled=True)


def integrate_parcels(owner, rank, live, answered, parcels, steps=4):
    size = BLK_DEV // steps
    block = pl.BlockSpec((5, size, LANES), lambda s: (0, s, 0))
    small = whole((CHUNKS, LANES))
    return pl.pallas_call(
        parcel_kernel,
        grid=(steps,),
        in_specs=[small, small, small, whole((DEVICES, LANES)), block],
        out_specs=[block, whole((DEVICES, LANES))],
        out_shape=[
            jax.ShapeDtypeStruct((5, BLK_DEV, LANES), F32),
            jax.ShapeDtypeStruct((DEVICES, LANES), F32),
        ],
        scratch_shapes=[
            pltpu.VMEM((LANES, LANES), BF16),
            pltpu.VMEM((LANES, PIECES * LANES), BF16),
            pltpu.VMEM((PIECES * LANES, NVAR * LANES), BF16),
            pltpu.VMEM((NVAR * LANES, LANES), BF16),
        ],
        compiler_params=compiler_params(),
    )(owner, rank, live, answered, parcels)


def body(gas_state, particle_blocks, owner, host_cell, live_count):
    gas, pair = lax.axis_index("gas"), lax.axis_index("grp")
    count = lax.axis_size("gas")
    owner = owner.reshape(CHUNKS, LANES)
    host_cell = host_cell.reshape(CHUNKS, LANES)
    live = live_count.reshape(CHUNKS, LANES)
    square = jax.ShapeDtypeStruct((DEVICES, LANES), F32)

    requests, rank = call(
        request_kernel,
        [
            jax.ShapeDtypeStruct((DEVICES, LANES), jnp.int32),
            jax.ShapeDtypeStruct((CHUNKS, LANES), jnp.int32),
        ],
    )(owner, host_cell)
    asked = deliver(requests)

    edge = lax.dynamic_slice_in_dim(gas_state, (1 - pair) * (CY - 8), 8, axis=2)
    edge = lax.ppermute(edge, "grp", [(0, 1), (1, 0)])
    upward = jnp.concatenate([gas_state[:, CX - HALO :], edge[:, CX - HALO :]], axis=2)
    downward = jnp.concatenate([gas_state[:, :HALO], edge[:, :HALO]], axis=2)
    low = lax.ppermute(upward, "gas", [(i, (i + 1) % count) for i in range(count)])
    high = lax.ppermute(downward, "gas", [((i + 1) % count, i) for i in range(count)])

    flat = gas_state.reshape(6, ROWS, NZ)
    table = call(
        table_kernel,
        jax.ShapeDtypeStruct((NVAR * LANES, PIECES * 2 * ROWS), BF16),
    )(flat)
    replies = call(gather_kernel, square, [pltpu.VMEM((LANES, LANES), F32)])(asked, table)
    answered = deliver(replies)

    parcels_next, sources = integrate_parcels(owner, rank, live, answered, particle_blocks)
    come = deliver(sources)

    place = jnp.stack([pair, gas == 0, gas == count - 1]).astype(jnp.int32)
    extended = pltpu.VMEM((6, EXT_X, EXT_Y, NZ), F32)
    vmem = pl.BlockSpec(memory_space=pltpu.VMEM)
    section_three = call(
        gas_kernel,
        jax.ShapeDtypeStruct((6, CX, CY, NZ), F32),
        [
            extended,
            extended,
            extended,
            pltpu.VMEM((4, EXT_X, EXT_Y, NZ), F32),
            pltpu.VMEM((6, EXT_Y, NZ), F32),
        ],
        in_specs=[pl.BlockSpec(memory_space=pltpu.SMEM)] + [vmem] * 4,
    )(place, gas_state, edge, low, high)

    gas_next = call(
        scatter_kernel,
        jax.ShapeDtypeStruct((6, ROWS, NZ), F32),
        [pltpu.VMEM((NVAR * LANES, 2 * ROWS), F32)],
    )(asked, come, section_three.reshape(6, ROWS, NZ))
    return (gas_next.reshape(6, CX, CY, NZ), parcels_next)


def solution(mesh):
    placed = (
        P(None, "gas", "grp", None),
        P(None, AXES, None),
        P(AXES, None),
        P(AXES),
        P(AXES),
    )
    return jax.shard_map(
        body,
        mesh=mesh,
        in_specs=placed,
        out_specs=(P(None, "gas", "grp", None), P(None, AXES, None)),
        check_vma=False,
    )
```

profile of v0, /device:TPU:1, one launch (start us, length us, event | category | flops | bytes accessed | tf_op | source)
XLA Modules:
  0.0 83.6 jit_solution(13563540309868395482)
XLA Ops:
  0.6 0.9 %constant_dynamic-slice_fusion = f32[6,4,8,256]{3,2,1,0:T(8,128)S(1)} fusion(f32[6,4,32,256]{3,2,1,0:T(8,128)} %gas_ref.1, s32[]{:T(128)S(6)} %select_n.3), kind=kLoop, calls=%fused_computation.3 | loop fusion | bytes 393220 | tf_op jit(solution)/shard_map/dynamic_slice | solution.py:395
  1.6 0.0 copy-start.3
  1.6 0.0 copy-start.5
  1.6 0.0 copy-start
  1.6 1.5 %collective-permute-start = (f32[6,4,8,256]{3,2,1,0:T(8,128)S(1)}, f32[6,4,8,256]{3,2,1,0:T(8,128)S(1)}, u32[]{:S(2)}, u32[]{:S(2)}) collective-permute-start(f32[6,4,8,256]{3,2,1,0:T(8,128)S(1)} %constant_dynamic-slice_fusion), channel_id=1, source_target_pairs={{0,1},{1,0},{2,3},{3,2},{4,5},{5,4},{6,7},{7,6},{8,9},{9,8},{10,11... | collective-permute-start | bytes 589832 | tf_op jit(solution)/shard_map/ppermute | solution.py:396
  3.1 1.3 %fusion = (f32[6,3,32,256]{3,2,1,0:T(8,128)S(1)}, f32[6,3,32,256]{3,2,1,0:T(8,128)S(1)}) fusion(f32[6,4,32,256]{3,2,1,0:T(8,128)} %gas_ref.1), kind=kLoop, calls=%fused_computation.4 | loop fusion | bytes 2359296 | tf_op jit(solution)/shard_map/slice | solution.py:398
  4.5 0.0 collective-permute-done.edge_ref
  4.5 0.9 %pad_maximum_fusion = f32[6,3,40,256]{3,2,1,0:T(8,128)} fusion(f32[6,3,8,256]{3,2,1,0:T(8,128)S(1)} %get-tuple-element.13, f32[6,3,32,256]{3,2,1,0:T(8,128)S(1)} %get-tuple-element.11), kind=kLoop, calls=%fused_computation | loop fusion | flops 184320 | bytes 1474560 | tf_op jit(solution)/shard_map/concatenate | solution.py:397
  5.4 0.0 copy-start.4
  5.5 1.7 %collective-permute-start.1 = (f32[6,3,40,256]{3,2,1,0:T(8,128)}, f32[6,3,40,256]{3,2,1,0:T(8,128)S(1)}, u32[]{:S(2)}, u32[]{:S(2)}) collective-permute-start(f32[6,3,40,256]{3,2,1,0:T(8,128)} %pad_maximum_fusion), channel_id=1, source_target_pairs={{0,2},{2,4},{4,6},{6,8},{8,10},{10,12},{12,14},{14,16},{16,18},{18... | collective-permute-start | bytes 2211848 | tf_op jit(solution)/shard_map/ppermute | solution.py:399
  7.2 1.0 %pad_maximum_fusion.1 = f32[6,3,40,256]{3,2,1,0:T(8,128)} fusion(f32[6,3,8,256]{3,2,1,0:T(8,128)S(1)} %get-tuple-element.12, f32[6,3,32,256]{3,2,1,0:T(8,128)S(1)} %get-tuple-element.10), kind=kLoop, calls=%fused_computation.1 | loop fusion | flops 184320 | bytes 1474560 | tf_op jit(solution)/shard_map/concatenate | solution.py:398
  8.1 6.8 %collective-permute-start.2 = (f32[6,3,40,256]{3,2,1,0:T(8,128)}, f32[6,3,40,256]{3,2,1,0:T(8,128)S(1)}, u32[]{:S(2)}, u32[]{:S(2)}) collective-permute-start(f32[6,3,40,256]{3,2,1,0:T(8,128)} %pad_maximum_fusion.1), channel_id=1, source_target_pairs={{2,0},{4,2},{6,4},{8,6},{10,8},{12,10},{14,12},{16,14},{18,16},{20... | collective-permute-start | bytes 2211848 | tf_op jit(solution)/shard_map/ppermute | solution.py:400
  14.9 0.0 copy-done.3
  14.9 0.0 copy-done.5
  14.9 1.8 %shard_map.68 = (s32[128,128]{1,0:T(8,128)}, s32[8,128]{1,0:T(8,128)S(1)}) custom-call(s32[8,128]{1,0:T(8,128)S(1)} %bitcast.28, s32[8,128]{1,0:T(8,128)S(1)} %bitcast.31), custom_call_target="tpu_custom_call" | custom-call | tf_op jit(solution)/shard_map/pallas_call | solution.py:386
  16.8 3.7 %all-to-all-start = ((s32[128,1,128]{2,1,0:T(1,128)}), s32[128,1,128]{2,1,0:T(1,128)S(1)}, u32[]{:S(2)}, u32[]{:S(2)}) async-start(s32[128,1,128]{2,1,0:T(1,128)} %bitcast.3), calls=%async_computation | async-start | bytes 131072 | tf_op jit(solution)/shard_map/all_to_all | solution.py:352
  20.5 0.0 copy-done
  20.5 0.3 shard_map.69.table_ref
  20.8 11.3 %all-to-all-done = s32[128,1,128]{2,1,0:T(1,128)S(1)} async-done(((s32[128,1,128]{2,1,0:T(1,128)}), s32[128,1,128]{2,1,0:T(1,128)S(1)}, u32[]{:S(2)}, u32[]{:S(2)}) %all-to-all-start) | async-done | bytes 65568 | tf_op jit(solution)/shard_map/all_to_all | solution.py:352
  32.1 2.4 %shard_map.70 = f32[128,128]{1,0:T(8,128)S(1)} custom-call(s32[128,128]{1,0:T(8,128)S(1)} %bitcast.23, bf16[640,768]{1,0:T(8,128)(2,1)S(1)} %shard_map.69.table_ref), custom_call_target="tpu_custom_call" | custom-call | tf_op jit(solution)/shard_map/pallas_call | solution.py:407
  34.5 0.0 copy-start.2
  34.5 0.6 copy-done.2
  35.2 10.1 %all-to-all-start.1 = ((f32[128,1,128]{2,1,0:T(1,128)}), f32[128,1,128]{2,1,0:T(1,128)S(1)}, u32[]{:S(2)}, u32[]{:S(2)}) async-start(f32[128,1,128]{2,1,0:T(1,128)} %bitcast.25), calls=%async_computation.1 | async-start | bytes 131072 | tf_op jit(solution)/shard_map/all_to_all | solution.py:352
  45.3 9.3 %all-to-all-done.1 = f32[128,1,128]{2,1,0:T(1,128)S(1)} async-done(((f32[128,1,128]{2,1,0:T(1,128)}), f32[128,1,128]{2,1,0:T(1,128)S(1)}, u32[]{:S(2)}, u32[]{:S(2)}) %all-to-all-start.1) | async-done | bytes 65568 | tf_op jit(solution)/shard_map/all_to_all | solution.py:352
  54.6 0.0 copy-done.4
  54.6 0.0 copy-start.1
  54.6 1.7 %copy-done.1 = f32[5,1024,128]{2,1,0:T(8,128)S(1)} copy-done((f32[5,1024,128]{2,1,0:T(8,128)S(1)}, f32[5,1024,128]{2,1,0:T(8,128)}, u32[]{:S(2)}) %copy-start.1) | copy-done | bytes 2621464
  56.3 9.6 %shard_map.71 = (f32[5,1024,128]{2,1,0:T(8,128)}, f32[128,128]{1,0:T(8,128)}) custom-call(s32[8,128]{1,0:T(8,128)S(1)} %bitcast.29, s32[8,128]{1,0:T(8,128)S(1)} %get-tuple-element.7.rank_ref, s32[8,128]{1,0:T(8,128)S(1)} %bitcast.30, f32[128,128]{1,0:T(8,128)S(1)} %bitcast.27, f32[5,1024,128]{2,1,0:T(8,128)S(1)} %copy-done.1), custom_call_target="tpu_custom_call" | custom-call | tf_op jit(solution)/shard_map/pallas_call | solution.py:359
  65.9 4.6 %all-to-all-start.2 = ((f32[128,1,128]{2,1,0:T(1,128)}), f32[128,1,128]{2,1,0:T(1,128)S(1)}, u32[]{:S(2)}, u32[]{:S(2)}) async-start(f32[128,1,128]{2,1,0:T(1,128)} %bitcast.11), calls=%async_computation.2 | async-start | bytes 131072 | tf_op jit(solution)/shard_map/all_to_all | solution.py:352
  70.6 0.1 pad_add_fusion.place_ref
  70.6 0.0 collective-permute-done.1.low_ref
  70.6 0.0 collective-permute-done.2.high_ref
  70.6 9.7 %shard_map.72 = f32[6,4,32,256]{3,2,1,0:T(8,128)S(1)} custom-call(s32[3]{0:T(128)S(1)} %pad_add_fusion.place_ref, f32[6,4,32,256]{3,2,1,0:T(8,128)S(1)} %copy-done, f32[6,4,8,256]{3,2,1,0:T(8,128)S(1)} %collective-permute-done.edge_ref, f32[6,3,40,256]{3,2,1,0:T(8,128)S(1)} %collective-permute-done.1.low_ref, ...), custom_call_target="tpu_custom_call" | custom-call | tf_op jit(solution)/shard_map/pallas_call | solution.py:416
  80.3 0.0 all-to-all-done.2
  80.3 3.3 %shard_map.73 = f32[6,128,256]{2,1,0:T(8,128)} custom-call(s32[128,128]{1,0:T(8,128)S(1)} %bitcast.24, f32[128,128]{1,0:T(8,128)S(1)} %bitcast.26, f32[6,128,256]{2,1,0:T(8,128)S(1)} %bitcast.22), custom_call_target="tpu_custom_call" | custom-call | tf_op jit(solution)/shard_map/pallas_call | solution.py:429
  (1 shorter events, 0.0 us)
Async XLA Ops:
  1.6 13.3 %copy-start.3 = (s32[1024,1]{0,1:T(1,128)S(1)}, s32[1024,1]{0,1:T(1,128)}, u32[]{:S(2)}) copy-start(s32[1024,1]{0,1:T(1,128)} %param.7) | copy-start | bytes 12292
  1.6 13.3 %copy-start.5 = (s32[1024]{0:T(1024)S(1)}, s32[1024]{0:T(1024)}, u32[]{:S(2)}) copy-start(s32[1024]{0:T(1024)} %param.8) | copy-start | bytes 12292
  1.6 18.9 %copy-start = (f32[6,4,32,256]{3,2,1,0:T(8,128)S(1)}, f32[6,4,32,256]{3,2,1,0:T(8,128)}, u32[]{:S(2)}) copy-start(f32[6,4,32,256]{3,2,1,0:T(8,128)} %gas_ref.1) | copy-start | bytes 2359300
  1.6 2.9 %collective-permute-start = (f32[6,4,8,256]{3,2,1,0:T(8,128)S(1)}, f32[6,4,8,256]{3,2,1,0:T(8,128)S(1)}, u32[]{:S(2)}, u32[]{:S(2)}) collective-permute-start(f32[6,4,8,256]{3,2,1,0:T(8,128)S(1)} %constant_dynamic-slice_fusion), channel_id=1, source_target_pairs={{0,1},{1,0},{2,3},{3,2},{4,5},{5,4},{6,7},{7,6},{8,9},{9,8},{10,11... | collective-permute-start | bytes 589832 | tf_op jit(solution)/shard_map/ppermute | solution.py:396
  5.4 49.1 %copy-start.4 = (s32[1024]{0:T(1024)S(1)}, s32[1024]{0:T(1024)}, u32[]{:S(2)}) copy-start(s32[1024]{0:T(1024)} %param.9) | copy-start | bytes 12292
  5.5 65.2 %collective-permute-start.1 = (f32[6,3,40,256]{3,2,1,0:T(8,128)}, f32[6,3,40,256]{3,2,1,0:T(8,128)S(1)}, u32[]{:S(2)}, u32[]{:S(2)}) collective-permute-start(f32[6,3,40,256]{3,2,1,0:T(8,128)} %pad_maximum_fusion), channel_id=1, source_target_pairs={{0,2},{2,4},{4,6},{6,8},{8,10},{10,12},{12,14},{14,16},{16,18},{18... | collective-permute-start | bytes 2211848 | tf_op jit(solution)/shard_map/ppermute | solution.py:399
  8.1 62.5 %collective-permute-start.2 = (f32[6,3,40,256]{3,2,1,0:T(8,128)}, f32[6,3,40,256]{3,2,1,0:T(8,128)S(1)}, u32[]{:S(2)}, u32[]{:S(2)}) collective-permute-start(f32[6,3,40,256]{3,2,1,0:T(8,128)} %pad_maximum_fusion.1), channel_id=1, source_target_pairs={{2,0},{4,2},{6,4},{8,6},{10,8},{12,10},{14,12},{16,14},{18,16},{20... | collective-permute-start | bytes 2211848 | tf_op jit(solution)/shard_map/ppermute | solution.py:400
  16.8 15.3 %all-to-all-start = ((s32[128,1,128]{2,1,0:T(1,128)}), s32[128,1,128]{2,1,0:T(1,128)S(1)}, u32[]{:S(2)}, u32[]{:S(2)}) async-start(s32[128,1,128]{2,1,0:T(1,128)} %bitcast.3), calls=%async_computation | async-start | bytes 131072 | tf_op jit(solution)/shard_map/all_to_all | solution.py:352
  34.5 0.6 copy-start.2
  35.2 19.4 %all-to-all-start.1 = ((f32[128,1,128]{2,1,0:T(1,128)}), f32[128,1,128]{2,1,0:T(1,128)S(1)}, u32[]{:S(2)}, u32[]{:S(2)}) async-start(f32[128,1,128]{2,1,0:T(1,128)} %bitcast.25), calls=%async_computation.1 | async-start | bytes 131072 | tf_op jit(solution)/shard_map/all_to_all | solution.py:352
  54.6 1.7 %copy-start.1 = (f32[5,1024,128]{2,1,0:T(8,128)S(1)}, f32[5,1024,128]{2,1,0:T(8,128)}, u32[]{:S(2)}) copy-start(f32[5,1024,128]{2,1,0:T(8,128)} %old_ref.1) | copy-start | bytes 7864324
  65.9 14.4 %all-to-all-start.2 = ((f32[128,1,128]{2,1,0:T(1,128)}), f32[128,1,128]{2,1,0:T(1,128)S(1)}, u32[]{:S(2)}, u32[]{:S(2)}) async-start(f32[128,1,128]{2,1,0:T(1,128)} %bitcast.11), calls=%async_computation.2 | async-start | bytes 131072 | tf_op jit(solution)/shard_map/all_to_all | solution.py:352
where the time goes:
time: 83.9 us; the launch traced here: 83.6 us
  starting transfers between devices  28.4 us (34%)
  Pallas kernels  27.1 us (32%)
  waiting for transfers between devices  20.6 us (25%)
  local copies, waits for them, and re-layouts  4.7 us (6%)
  other arithmetic  1.97 us (2%)
    all_to_all x3, waiting for transfers between devices, deliver(): return lax.all_to_all(buffer, AXES, split_axis=0, concat_axis=0, tiled=True)  20.6 us
    all_to_all x3, starting transfers between devices, deliver(): return lax.all_to_all(buffer, AXES, split_axis=0, concat_axis=0, tiled=True)  18.4 us
    pallas_call x1, Pallas kernels, body(): call(gas_kernel, jax.ShapeDtypeStruct((6, CX, CY, NZ), F32), [extended, e...  9.66 us
    pallas_call x1, Pallas kernels, integrate_parcels(): pl.pallas_call(parcel_kernel, grid=(steps,), in_specs=[small, small, smal...  9.62 us
    ppermute x1, starting transfers between devices, body(): lax.ppermute(downward, 'gas', [((i + 1) % count, i) for i in range(count)])  6.77 us
    pallas_call x1, Pallas kernels, body(): call(scatter_kernel, jax.ShapeDtypeStruct((6, ROWS, NZ), F32), [pltpu.VME...  3.26 us
    pallas_call x1, Pallas kernels, body(): call(gather_kernel, square, [pltpu.VMEM((LANES, LANES), F32)])(asked, table)  2.44 us
    unnamed x12, local copies, waits for them, and re-layouts  2.39 us
  transfers between devices with their start and end apart: 6, of which 2 were waited for; matrix products, arithmetic and copies ran while one was open for 3% of the time, Pallas kernels for 28%

commit v1 on v0

v1 whole, which is shorter than its diff:
```python
import jax
import jax.numpy as jnp
from jax import lax
from jax.experimental import pallas as pl
from jax.experimental.pallas import tpu as pltpu
from jax.sharding import PartitionSpec as P

AXES = ("gas", "grp")
DEVICES = 128
LANES = 128
CAP = 16
CX, CY, NZ = 4, 32, 256
ROWS = CX * CY
BLK_DEV = 1024
CHUNKS = BLK_DEV // LANES
NSUB = 4
NVAR = 5
PIECES = 3
HALO = 3
PART = 256
PARCEL_FLOPS = 10**10
EXT_X = CX + 2 * HALO
EXT_Y = CY + 8

LAM = 0.1
GAMMA_ADIABATIC = 1.4
CLOCK_INCREMENT = 0.25
TAU_DRAG = 0.8
THERMAL_RELAX = 1.2
EVAP_RATE = 0.5
LATENT_EVAPORATE = 0.3
WEIGHT = 0.05
LOG2E = 1.4426950408889634

F32 = jnp.float32
BF16 = jnp.bfloat16
MIB = 1024 * 1024


def iota(shape, dim):
    return lax.broadcasted_iota(jnp.int32, shape, dim)


def dot(a, b):
    return lax.dot_general(a, b, (((1,), (0,)), ((), ())), preferred_element_type=F32)


def dot_nt(a, b):
    return lax.dot_general(a, b, (((1,), (1,)), ((), ())), preferred_element_type=F32)


def split(x):
    pieces = []
    for _ in range(PIECES):
        piece = x.astype(BF16)
        pieces.append(piece)
        x = x - piece.astype(F32)
    return pieces


def ones_where(mask):
    return jnp.where(mask, 1.0, 0.0).astype(BF16)


def compiler_params(mib):
    return pltpu.CompilerParams(vmem_limit_bytes=mib * MIB)


def request_kernel(owner_ref, cell_ref, req_ref, rank_ref):
    down = iota((LANES, LANES), 0)
    across = iota((LANES, 2 * LANES), 1)
    earlier = ones_where((iota((LANES, 2 * LANES), 0) < across) | (across >= LANES))
    named = [down == owner_ref[i : i + 1, :] for i in range(CHUNKS)]
    hots = [ones_where(n) for n in named]
    counts = dot(jnp.concatenate(hots, axis=0), earlier)
    before = jnp.zeros((LANES, LANES), F32)
    slots = iota((CAP, LANES), 0)
    highs, lows = [], []
    for i in range(CHUNKS):
        count = counts[i * LANES : (i + 1) * LANES]
        place = jnp.where(named[i], count[:, :LANES] + before, 0.0)
        rank = jnp.sum(place, axis=0, keepdims=True).astype(jnp.int32)
        rank_ref[i : i + 1, :] = rank
        before = before + count[:, LANES:]
        cell = cell_ref[i : i + 1, :]
        placed = slots == rank
        highs.append(jnp.where(placed, (((cell >> 8) + 1) << 8).astype(F32), 0.0))
        lows.append(jnp.where(placed, (cell & 255).astype(F32), 0.0))
    values = jnp.concatenate(highs + lows, axis=1).astype(BF16)
    total = dot_nt(jnp.concatenate(hots + hots, axis=1), values)
    req_ref[...] = jnp.full((DEVICES, LANES), -1, jnp.int32)
    req_ref[:, :CAP] = total.astype(jnp.int32) - 256


def outward_kernel(gas_ref, edge_ref, table_ref, up_ref, down_ref):
    inverse = 1.0 / gas_ref[0].reshape(ROWS, NZ)
    for c in range(NVAR):
        value = gas_ref[1 + c].reshape(ROWS, NZ) * inverse
        for half in range(2):
            turned = value[:, half * LANES : (half + 1) * LANES].T
            for p, piece in enumerate(split(turned)):
                start = p * 2 * ROWS + half * ROWS
                table_ref[c * LANES : (c + 1) * LANES, start : start + ROWS] = piece
    for i in range(HALO):
        here = slice(i * CY, (i + 1) * CY)
        up_ref[:, here, :] = gas_ref[:, CX - HALO + i]
        down_ref[:, here, :] = gas_ref[:, i]
    at = HALO * CY

    def corners(near, after):
        for ref, one, two in ((up_ref, CX - 1, CX - 2), (down_ref, 0, 1)):
            ref[:, at : at + 8, :] = jnp.zeros((6, 8, NZ), F32)
            ref[:, at : at + 1, :] = edge_ref[:, one, near : near + 1, :]
            ref[:, at + 1 : at + 2, :] = edge_ref[:, one, after : after + 1, :]
            ref[:, at + 2 : at + 3, :] = edge_ref[:, two, near : near + 1, :]

    pair = lax.axis_index("grp")
    pl.when(pair == 0)(lambda: corners(0, 1))
    pl.when(pair == 1)(lambda: corners(7, 6))


def cell_parts(asked_ref):
    cell = asked_ref[...].astype(F32).T.astype(jnp.int32)
    return (cell >> 8) + ROWS * ((cell >> 7) & 1), cell & (LANES - 1)


def gather_kernel(asked_ref, table_ref, reply_ref, found):
    row, lane = cell_parts(asked_ref)
    table = table_ref[...]
    found[...] = jnp.zeros((LANES, LANES), F32)
    for pair in range(CAP // 2):
        k = 2 * pair
        rows = jnp.concatenate([row[k : k + 1], row[k + 1 : k + 2]], axis=1)
        lanes = jnp.concatenate([lane[k : k + 1], lane[k + 1 : k + 2]], axis=1)
        hot = ones_where(iota((2 * ROWS, 2 * LANES), 0) == rows)
        values = dot(table, jnp.concatenate([hot] * PIECES, axis=0))
        here = iota((LANES, 2 * LANES), 0) == lanes
        for c in range(NVAR):
            part = values[c * LANES : (c + 1) * LANES]
            picked = jnp.sum(jnp.where(here, part, 0.0), axis=0, keepdims=True)
            found[c * CAP + k : c * CAP + k + 1, :] = picked[:, :LANES]
            found[c * CAP + k + 1 : c * CAP + k + 2, :] = picked[:, LANES:]
    reply_ref[...] = found[...].T


def integrate(parcels, gas_vars):
    mass, speeds, thermal = parcels[0], parcels[1:4], parcels[4]
    ambient, vapor = gas_vars[3], gas_vars[4]
    power = first_power = (-2.0 / 3.0) * jnp.log2(mass)
    exposure = None
    rate = CLOCK_INCREMENT * EVAP_RATE * LOG2E
    headroom = rate * (0.3 - vapor)
    offset = ambient + LATENT_EVAPORATE
    for _ in range(NSUB):
        inverse = jnp.exp2(power)
        square = 1.0 + thermal * thermal
        guess = pl.reciprocal(square, approx=True)
        guess = guess * (2.0 - square * guess)
        loss = (headroom - (0.3 * rate) * guess) * inverse
        kept = jnp.exp2((-CLOCK_INCREMENT / THERMAL_RELAX * LOG2E) * inverse)
        thermal = offset + (thermal - ambient) * kept - LATENT_EVAPORATE * jnp.exp2(loss)
        power = power + (2.0 / 3.0) * loss
        exposure = inverse if exposure is None else exposure + inverse
    drag = jnp.exp2((-CLOCK_INCREMENT / TAU_DRAG * LOG2E) * exposure)
    moved = [gas_vars[c] + (speeds[c] - gas_vars[c]) * drag for c in range(3)]
    return [mass * jnp.exp2(1.5 * (first_power - power))] + moved + [thermal]


def parcel_kernel(
    owner_ref, rank_ref, live_ref, ans_ref, old_ref, new_ref, send_ref,
    held, made, hot, turned, slots, alive, spread, placed, answered, got, sent, arrived,
):
    parts = BLK_DEV // PART
    asking = pltpu.make_async_copy(ans_ref, answered, arrived)
    asking.start()
    fetches = []
    for part in range(parts):
        here = slice(part * PART, (part + 1) * PART)
        fetches.append(pltpu.make_async_copy(old_ref.at[:, here, :], held.at[:, here, :], got.at[part]))
        fetches[part].start()

    pad = jnp.zeros((LANES - 3 * CHUNKS, LANES), F32)
    rows = [owner_ref[...], rank_ref[...], live_ref[...]]
    stack = jnp.concatenate([r.astype(F32) for r in rows] + [pad], axis=0)
    columns = stack.T.astype(BF16)
    across = iota((LANES, LANES), 1)
    down = iota((LANES, LANES), 0)
    for i in range(CHUNKS):
        shape = (LANES, 3 * LANES)
        chosen = ones_where(iota(shape, 0) == i + CHUNKS * (iota(shape, 1) // LANES))
        wide = dot(columns, chosen).astype(jnp.int32)
        owner, rank, live = (wide[:, s * LANES : (s + 1) * LANES] for s in range(3))
        here = slice(i * LANES, (i + 1) * LANES)
        hot[here, :] = ones_where(owner == across)
        slots[here, :] = ones_where(across % CAP == rank)
        alive[here, :] = jnp.where(across < live, 1.0, 0.0)
        turned[:, here] = ones_where(down == owner_ref[i : i + 1, :])
    shape = (PIECES * LANES, NVAR * LANES)
    spread[...] = ones_where((iota(shape, 0) % LANES) // CAP == iota(shape, 1) // LANES)

    asking.wait()
    answers = jnp.concatenate(split(answered[...]), axis=1)
    kind = iota((PART, LANES), 1) // CAP
    stores = []
    for part in range(parts):
        here = slice(part * PART, (part + 1) * PART)
        slot = slots[here, :]
        received = dot(hot[here, :], answers).astype(BF16)
        wide = dot(received * jnp.concatenate([slot] * PIECES, axis=1), spread[...])
        gas_vars = [wide[:, c * LANES : (c + 1) * LANES] for c in range(NVAR)]
        fetches[part].wait()
        old = [held[c, here, :] for c in range(5)]
        living = alive[here, :] > 0.0
        new = [jnp.where(living, n, o) for n, o in zip(integrate(old, gas_vars), old)]
        for c in range(5):
            made[c, here, :] = new[c]
        stores.append(pltpu.make_async_copy(made.at[:, here, :], new_ref.at[:, here, :], sent.at[part]))
        stores[part].start()
        change = [old[0] - new[0]] + [old[0] * old[c] - new[0] * new[c] for c in range(1, 5)]
        total = jnp.zeros((PART, LANES), F32)
        for c in range(NVAR):
            total = jnp.where(kind == c, jnp.sum(change[c], axis=1, keepdims=True), total)
        for p, piece in enumerate(split(total)):
            placed[here, p * LANES : (p + 1) * LANES] = piece * slot
    send = dot(turned[...], placed[...])
    send_ref[...] = sum(send[:, p * LANES : (p + 1) * LANES] for p in range(PIECES))
    for store in stores:
        store.wait()


def scatter_kernel(asked_ref, come_ref, section_ref, out_ref, total):
    row, lane = cell_parts(asked_ref)
    pieces = [p.astype(F32) for p in split(come_ref[...].T)]
    for pair in range(CAP // 2):
        hots, parts = [], []
        for k in (2 * pair, 2 * pair + 1):
            hot = ones_where(iota((2 * ROWS, LANES), 0) == row[k : k + 1])
            here = iota((LANES, LANES), 0) == lane[k : k + 1]
            for piece in pieces:
                hots.append(hot)
                parts.append(
                    jnp.concatenate(
                        [
                            jnp.where(here, piece[c * CAP + k : c * CAP + k + 1], 0.0)
                            for c in range(NVAR)
                        ],
                        axis=0,
                    ).astype(BF16)
                )
        added = dot_nt(jnp.concatenate(parts, axis=1), jnp.concatenate(hots, axis=1))
        if pair == 0:
            total[...] = added
        else:
            total[...] += added
    for c in range(NVAR):
        for half in range(2):
            cells = WEIGHT * total[c * LANES : (c + 1) * LANES, half * ROWS : (half + 1) * ROWS].T
            z = slice(half * LANES, (half + 1) * LANES)
            out_ref[c, :, z] = section_ref[c, :, z] + cells
            if c == 0:
                out_ref[NVAR, :, z] = section_ref[NVAR, :, z] + cells


def gas_kernel(gas_ref, edge_ref, low_ref, high_ref, out_ref, q0, q1, q2, prim, face):
    place, pair = lax.axis_index("gas"), lax.axis_index("grp")
    own = pl.ds(pl.multiple_of(pair * 8, 8), CY)
    side = pl.ds(pl.multiple_of((1 - pair) * CY, 8), 8)
    inner = slice(HALO, HALO + CX)
    q0[:, inner, own, :] = gas_ref[...]
    q0[:, inner, side, :] = edge_ref[...]
    for i in range(HALO):
        q0[:, i, own, :] = low_ref[:, i * CY : (i + 1) * CY, :]
        q0[:, HALO + CX + i, own, :] = high_ref[:, i * CY : (i + 1) * CY, :]

    def corners(near, after):
        at = HALO * CY
        for ref, one, two in ((low_ref, HALO - 1, HALO - 2), (high_ref, HALO + CX, HALO + CX + 1)):
            q0[:, one, near : near + 1, :] = ref[:, at : at + 1, :]
            q0[:, one, after : after + 1, :] = ref[:, at + 1 : at + 2, :]
            q0[:, two, near : near + 1, :] = ref[:, at + 2 : at + 3, :]

    pl.when(pair == 0)(lambda: corners(CY, CY + 1))
    pl.when(pair == 1)(lambda: corners(7, 6))

    def ghosts(q):
        @pl.when(place == 0)
        def _():
            q[:, HALO - 1] = q[:, HALO]

        @pl.when(place == lax.axis_size("gas") - 1)
        def _():
            q[:, HALO + CX] = q[:, HALO + CX - 1]

    row_in_tile = iota((8, NZ), 0)
    lane = iota((EXT_Y, LANES), 1)

    def above(v, axis):
        if axis == 0:
            moved = pltpu.roll(v, EXT_Y - 1, 0)
            tail = jnp.where(row_in_tile == 7, v[EXT_Y - 8 :], moved[EXT_Y - 8 :])
            return jnp.concatenate([moved[: EXT_Y - 8], tail], axis=0)
        left, right = v[:, :LANES], v[:, LANES:]
        left_moved, right_moved = pltpu.roll(left, LANES - 1, 1), pltpu.roll(right, LANES - 1, 1)
        at_end = lane == LANES - 1
        return jnp.concatenate(
            [jnp.where(at_end, right_moved, left_moved), jnp.where(at_end, right, right_moved)], axis=1
        )

    def below(g, first, axis):
        if axis == 0:
            moved = pltpu.roll(g, 1, 0)
            head = jnp.where(row_in_tile == 0, first, moved[:8])
            return jnp.concatenate([head, moved[8:]], axis=0)
        left, right = pltpu.roll(g[:, :LANES], 1, 1), pltpu.roll(g[:, LANES:], 1, 1)
        at_start = lane == 0
        return jnp.concatenate(
            [jnp.where(at_start, first, left), jnp.where(at_start, left, right)], axis=1
        )

    def primitives(q, x):
        inverse = 1.0 / q[0, x]
        for d in range(3):
            prim[d, x] = q[1 + d, x] * inverse
        prim[3, x] = jnp.sqrt(GAMMA_ADIABATIC * (q[4, x] * inverse))

    def x_faces(q, x):
        u, un = prim[0, x], prim[0, x + 1]
        rate = jnp.maximum(jnp.abs(u) + prim[3, x], jnp.abs(un) + prim[3, x + 1])
        here, there = u + rate, un - rate
        faces = []
        for c in range(6):
            g = q[c, x] * here + q[c, x + 1] * there
            faces.append(g + (q[4, x] + q[4, x + 1]) if c == 1 else g)
        return faces

    def update(q, combine, start, stop):
        def fill(x, carry):
            primitives(q, x)
            return carry

        lax.fori_loop(start - 1, stop + 1, fill, 0)
        for c, value in enumerate(x_faces(q, start - 1)):
            face[c] = value

        def row(x, carry):
            change = []
            for c, upper in enumerate(x_faces(q, x)):
                change.append(upper - face[c])
                face[c] = upper
            for axis in (0, 1):
                d = 1 + axis
                start_cells = (slice(0, 8), slice(None)) if axis == 0 else (slice(None), slice(0, LANES))
                u = prim[d, x]
                a = jnp.abs(u) + prim[3, x]
                un = above(u, axis)
                rate = jnp.maximum(a, above(a, axis))
                here, there = u + rate, un - rate
                for c in range(6):
                    v = q[c, x]
                    g = v * here + above(v, axis) * there
                    first = 2.0 * (v[start_cells] * u[start_cells])
                    if c == 1 + d:
                        p = q[4, x]
                        g = g + (p + above(p, axis))
                        first = first + 2.0 * p[start_cells]
                    change[c] = change[c] + (g - below(g, first, axis))
            for c in range(6):
                combine(c, x, q[c, x] - (0.5 * LAM) * change[c])
            return carry

        lax.fori_loop(start, stop, row, 0)

    ghosts(q0)

    def first_section(c, x, value):
        q1[c, x] = value

    update(q0, first_section, 1, EXT_X - 1)
    ghosts(q1)

    def second_section(c, x, value):
        q2[c, x] = 0.75 * q0[c, x] + 0.25 * value

    update(q1, second_section, 2, EXT_X - 2)
    ghosts(q2)

    def third_section(c, x, value):
        q1[c, x] = q0[c, x] * (1.0 / 3.0) + (2.0 / 3.0) * value

    update(q2, third_section, HALO, HALO + CX)
    out_ref[...] = q1[:, inner, own, :]


SMALL = pl.CostEstimate(flops=1, bytes_accessed=1, transcendentals=0)


def call(kernel, mib, outs, scratch=(), cost=SMALL, **more):
    return pl.pallas_call(
        kernel,
        out_shape=outs,
        scratch_shapes=list(scratch),
        compiler_params=compiler_params(mib),
        cost_estimate=cost,
        **more,
    )


def deliver(buffer):
    return lax.all_to_all(buffer, AXES, split_axis=0, concat_axis=0, tiled=True)


def integrate_parcels(owner, rank, live, answered, parcels):
    held = pl.BlockSpec(memory_space=pltpu.VMEM)
    far = pl.BlockSpec(memory_space=pl.ANY)
    return call(
        parcel_kernel,
        60,
        [
            jax.ShapeDtypeStruct((5, BLK_DEV, LANES), F32),
            jax.ShapeDtypeStruct((DEVICES, LANES), F32),
        ],
        [
            pltpu.VMEM((5, BLK_DEV, LANES), F32),
            pltpu.VMEM((5, BLK_DEV, LANES), F32),
            pltpu.VMEM((BLK_DEV, DEVICES), BF16),
            pltpu.VMEM((DEVICES, BLK_DEV), BF16),
            pltpu.VMEM((BLK_DEV, LANES), BF16),
            pltpu.VMEM((BLK_DEV, LANES), F32),
            pltpu.VMEM((PIECES * LANES, NVAR * LANES), BF16),
            pltpu.VMEM((BLK_DEV, PIECES * LANES), BF16),
            pltpu.VMEM((DEVICES, LANES), F32),
            pltpu.SemaphoreType.DMA((BLK_DEV // PART,)),
            pltpu.SemaphoreType.DMA((BLK_DEV // PART,)),
            pltpu.SemaphoreType.DMA,
        ],
        cost=pl.CostEstimate(flops=PARCEL_FLOPS, bytes_accessed=8 * 5 * BLK_DEV * LANES, transcendentals=0),
        in_specs=[held, held, held, far, far],
        out_specs=[far, held],
    )(owner, rank, live, answered, parcels)


def body(gas_state, particle_blocks, owner, host_cell, live_count):
    pair = lax.axis_index("grp")
    count = lax.axis_size("gas")
    owner = owner.reshape(CHUNKS, LANES)
    host_cell = host_cell.reshape(CHUNKS, LANES)
    live = live_count.reshape(CHUNKS, LANES)
    square = jax.ShapeDtypeStruct((DEVICES, LANES), F32)

    requests, rank = call(
        request_kernel,
        60,
        [
            jax.ShapeDtypeStruct((DEVICES, LANES), jnp.int32),
            jax.ShapeDtypeStruct((CHUNKS, LANES), jnp.int32),
        ],
    )(owner, host_cell)
    asked = deliver(requests)

    mine, _ = lax.optimization_barrier((gas_state, requests))
    edge = lax.dynamic_slice_in_dim(mine, (1 - pair) * (CY - 8), 8, axis=2)
    edge = lax.ppermute(edge, "grp", [(0, 1), (1, 0)])
    message = jax.ShapeDtypeStruct((6, HALO * CY + 8, NZ), F32)
    table, upward, downward = call(
        outward_kernel,
        12,
        [jax.ShapeDtypeStruct((NVAR * LANES, PIECES * 2 * ROWS), BF16), message, message],
    )(gas_state, edge)
    replies = call(gather_kernel, 16, square, [pltpu.VMEM((LANES, LANES), F32)])(asked, table)
    answered = deliver(replies)

    upward, downward, _ = lax.optimization_barrier((upward, downward, replies))
    low = lax.ppermute(upward, "gas", [(i, (i + 1) % count) for i in range(count)])
    high = lax.ppermute(downward, "gas", [((i + 1) % count, i) for i in range(count)])
    parcels_next, sources = integrate_parcels(owner, rank, live, answered, particle_blocks)
    come = deliver(sources)

    low, high, _ = lax.optimization_barrier((low, high, sources))
    extended = pltpu.VMEM((6, EXT_X, EXT_Y, NZ), F32)
    section_three = call(
        gas_kernel,
        28,
        jax.ShapeDtypeStruct((6, CX, CY, NZ), F32),
        [
            extended,
            extended,
            extended,
            pltpu.VMEM((4, EXT_X, EXT_Y, NZ), F32),
            pltpu.VMEM((6, EXT_Y, NZ), F32),
        ],
    )(gas_state, edge, low, high)

    gas_next = call(
        scatter_kernel,
        20,
        jax.ShapeDtypeStruct((6, ROWS, NZ), F32),
        [pltpu.VMEM((NVAR * LANES, 2 * ROWS), F32)],
    )(asked, come, section_three.reshape(6, ROWS, NZ))
    return (gas_next.reshape(6, CX, CY, NZ), parcels_next)


def solution(mesh):
    placed = (
        P(None, "gas", "grp", None),
        P(None, AXES, None),
        P(AXES, None),
        P(AXES),
        P(AXES),
    )
    return jax.shard_map(
        body,
        mesh=mesh,
        in_specs=placed,
        out_specs=(P(None, "gas", "grp", None), P(None, AXES, None)),
        check_vma=False,
    )
```

time: 83.9 us -> 67.7 us (0.81)
  waiting for transfers between devices: 20.6 us -> 10.2 us
  Pallas kernels: 27.1 us -> 24.8 us
  local copies, waits for them, and re-layouts: 4.7 us -> 2.69 us
  other arithmetic: 1.97 us -> 0 us
    all_to_all x3, waiting for transfers between devices: 20.6 us -> 9.58 us  [deliver(): return lax.all_to_all(buffer, AXES, split_axis=0, concat_axis=0, tiled=True)]
    pallas_call x6, Pallas kernels: 27.1 us -> 24.8 us  [the longest x1 7.75 us: body(): call(gas_kernel, 28, jax.ShapeDtypeStruct((6, CX, CY, NZ), F32), [extende...]
    concatenate x2 -> x0, other arithmetic: 1.9 us -> none  [the longest x1 0.96 us: body(): downward = jnp.concatenate([gas_state[:, :HALO], edge[:, :HALO]], axis=2)]
    slice x2 -> x0, local copies, waits for them, and re-layouts: 1.36 us -> none  [body(): downward = jnp.concatenate([gas_state[:, :HALO], edge[:, :HALO]], axis=2)]
    all_to_all x3, starting transfers between devices: 18.4 us -> 19.4 us  [deliver(): return lax.all_to_all(buffer, AXES, split_axis=0, concat_axis=0, tiled=True)]
    unnamed x12 -> x6, local copies, waits for them, and re-layouts: 2.39 us -> 1.75 us
  transfers between devices with their start and end apart: 6 -> 6, of which waited for: 2 -> 4; matrix products, arithmetic and copies ran while one was open for 3% -> 0% of each run, Pallas kernels for 28% -> 24%
where the time goes in v1:
time: 67.7 us; the launch traced here: 67.3 us
  starting transfers between devices  28.9 us (43%)
  Pallas kernels  24.8 us (37%)
  waiting for transfers between devices  10.2 us (15%)
  local copies, waits for them, and re-layouts  2.69 us (4%)
  between operations  0.7 us (1%)
    all_to_all x3, starting transfers between devices, deliver(): return lax.all_to_all(buffer, AXES, split_axis=0, concat_axis=0, tiled=True)  19.4 us
    all_to_all x3, waiting for transfers between devices, deliver(): return lax.all_to_all(buffer, AXES, split_axis=0, concat_axis=0, tiled=True)  9.58 us
    pallas_call x1, Pallas kernels, body(): call(gas_kernel, 28, jax.ShapeDtypeStruct((6, CX, CY, NZ), F32), [extende...  7.75 us
    pallas_call x1, Pallas kernels, integrate_parcels(): call(parcel_kernel, 60, [jax.ShapeDtypeStruct((5, BLK_DEV, LANES), F32),...  7.52 us
    ppermute x1, starting transfers between devices, body(): lax.ppermute(downward, 'gas', [((i + 1) % count, i) for i in range(count)])  6.3 us
    pallas_call x1, Pallas kernels, body(): call(scatter_kernel, 20, jax.ShapeDtypeStruct((6, ROWS, NZ), F32), [pltpu...  3.26 us
    pallas_call x1, Pallas kernels, body(): call(gather_kernel, 16, square, [pltpu.VMEM((LANES, LANES), F32)])  3.08 us
    pallas_call x1, Pallas kernels, body(): call(request_kernel, 60, [jax.ShapeDtypeStruct((DEVICES, LANES), jnp.int3...  2.05 us
  transfers between devices with their start and end apart: 6, of which 4 were waited for; matrix products, arithmetic and copies ran while one was open for 0% of the time, Pallas kernels for 24%

profile of v1, /device:TPU:1, one launch (start us, length us, event | category | flops | bytes accessed | tf_op | source)
XLA Modules:
  0.0 67.3 jit_solution(6944817668035206377)
XLA Ops:
  0.6 2.0 %shard_map.68 = (s32[128,128]{1,0:T(8,128)}, s32[8,128]{1,0:T(8,128)}) custom-call(s32[8,128]{1,0:T(8,128)} %bitcast.26, s32[8,128]{1,0:T(8,128)} %bitcast.25), custom_call_target="tpu_custom_call" | custom-call | flops 1 | bytes 1 | tf_op jit(solution)/shard_map/pallas_call | solution.py:450
  2.7 0.9 %constant_dynamic-slice_fusion = f32[6,4,8,256]{3,2,1,0:T(8,128)S(1)} fusion(f32[6,4,32,256]{3,2,1,0:T(8,128)} %gas_ref.3, s32[]{:T(128)S(6)} %select_n.3), kind=kLoop, calls=%fused_computation | loop fusion | bytes 393220 | tf_op jit(solution)/shard_map/dynamic_slice | solution.py:461
  3.6 1.5 %collective-permute-start = (f32[6,4,8,256]{3,2,1,0:T(8,128)S(1)}, f32[6,4,8,256]{3,2,1,0:T(8,128)S(1)}, u32[]{:S(2)}, u32[]{:S(2)}) collective-permute-start(f32[6,4,8,256]{3,2,1,0:T(8,128)S(1)} %constant_dynamic-slice_fusion), channel_id=1, source_target_pairs={{0,1},{1,0},{2,3},{3,2},{4,5},{5,4},{6,7},{7,6},{8,9},{9,8},{10,11... | collective-permute-start | bytes 589832 | tf_op jit(solution)/shard_map/ppermute | solution.py:462
  5.1 10.2 %all-to-all-start = ((s32[128,1,128]{2,1,0:T(1,128)}), s32[128,1,128]{2,1,0:T(1,128)S(1)}, u32[]{:S(2)}, u32[]{:S(2)}) async-start(s32[128,1,128]{2,1,0:T(1,128)} %bitcast.22), calls=%async_computation | async-start | bytes 131072 | tf_op jit(solution)/shard_map/all_to_all | solution.py:409
  15.3 0.0 collective-permute-done.edge_ref
  15.3 0.0 copy-start
  15.3 1.1 %copy-done = f32[6,4,32,256]{3,2,1,0:T(8,128)S(1)} copy-done((f32[6,4,32,256]{3,2,1,0:T(8,128)S(1)}, f32[6,4,32,256]{3,2,1,0:T(8,128)}, u32[]{:S(2)}) %copy-start) | copy-done | bytes 786456
  16.5 1.2 %shard_map.69 = (bf16[640,768]{1,0:T(8,128)(2,1)S(1)}, f32[6,104,256]{2,1,0:T(8,128)}, f32[6,104,256]{2,1,0:T(8,128)S(1)}) custom-call(f32[6,4,32,256]{3,2,1,0:T(8,128)S(1)} %copy-done, f32[6,4,8,256]{3,2,1,0:T(8,128)S(1)} %collective-permute-done.edge_ref), custom_call_target="tpu_custom_call" | custom-call | flops 1 | bytes 1 | tf_op jit(solution)/shard_map/pallas_call | solution.py:464
  17.6 7.0 %all-to-all-done = s32[128,1,128]{2,1,0:T(1,128)S(1)} async-done(((s32[128,1,128]{2,1,0:T(1,128)}), s32[128,1,128]{2,1,0:T(1,128)S(1)}, u32[]{:S(2)}, u32[]{:S(2)}) %all-to-all-start) | async-done | bytes 65568 | tf_op jit(solution)/shard_map/all_to_all | solution.py:409
  24.7 3.1 %shard_map.70 = f32[128,128]{1,0:T(8,128)} custom-call(s32[128,128]{1,0:T(8,128)S(1)} %bitcast.18, bf16[640,768]{1,0:T(8,128)(2,1)S(1)} %get-tuple-element.17.table_ref), custom_call_target="tpu_custom_call" | custom-call | flops 1 | bytes 1 | tf_op jit(solution)/shard_map/pallas_call | solution.py:469
  27.7 4.6 %all-to-all-start.1 = ((f32[128,1,128]{2,1,0:T(1,128)}), f32[128,1,128]{2,1,0:T(1,128)S(1)}, u32[]{:S(2)}, u32[]{:S(2)}) async-start(f32[128,1,128]{2,1,0:T(1,128)} %bitcast.7), calls=%async_computation.1 | async-start | bytes 131072 | tf_op jit(solution)/shard_map/all_to_all | solution.py:409
  32.4 1.7 %collective-permute-start.1 = (f32[6,104,256]{2,1,0:T(8,128)}, f32[6,104,256]{2,1,0:T(8,128)S(1)}, u32[]{:S(2)}, u32[]{:S(2)}) collective-permute-start(f32[6,104,256]{2,1,0:T(8,128)} %get-tuple-element.21), channel_id=1, source_target_pairs={{0,2},{2,4},{4,6},{6,8},{8,10},{10,12},{12,14},{14,16},{16,18},{18... | collective-permute-start | bytes 1916936 | tf_op jit(solution)/shard_map/ppermute | solution.py:473
  34.0 6.3 %collective-permute-start.2 = (f32[6,104,256]{2,1,0:T(8,128)S(1)}, f32[6,104,256]{2,1,0:T(8,128)S(1)}, u32[]{:S(2)}, u32[]{:S(2)}) collective-permute-start(f32[6,104,256]{2,1,0:T(8,128)S(1)} %get-tuple-element.22), channel_id=1, source_target_pairs={{2,0},{4,2},{6,4},{8,6},{10,8},{12,10},{14,12},{16,14},{18,16},{20... | collective-permute-start | bytes 1916936 | tf_op jit(solution)/shard_map/ppermute | solution.py:474
  40.3 1.5 %all-to-all-done.1 = f32[128,1,128]{2,1,0:T(1,128)S(1)} async-done(((f32[128,1,128]{2,1,0:T(1,128)}), f32[128,1,128]{2,1,0:T(1,128)S(1)}, u32[]{:S(2)}, u32[]{:S(2)}) %all-to-all-start.1) | async-done | bytes 65568 | tf_op jit(solution)/shard_map/all_to_all | solution.py:409
  41.8 0.0 copy-start.2
  41.8 0.6 copy-done.2
  42.4 0.0 copy-start.1
  42.4 7.5 %shard_map.71 = (f32[5,1024,128]{2,1,0:T(8,128)}, f32[128,128]{1,0:T(8,128)}) custom-call(s32[8,128]{1,0:T(8,128)} %bitcast.27, s32[8,128]{1,0:T(8,128)} %get-tuple-element.15.rank_ref, s32[8,128]{1,0:T(8,128)} %bitcast.28, f32[128,128]{1,0:T(8,128)} %bitcast.23, f32[5,1024,128]{2,1,0:T(8,128)} %old_ref.1), custom_call_target="tpu_custom_call" | custom-call | flops 10000000000 | bytes 5242880 | tf_op jit(solution)/shard_map/pallas_call | solution.py:415
  49.9 4.6 %all-to-all-start.2 = ((f32[128,1,128]{2,1,0:T(1,128)}), f32[128,1,128]{2,1,0:T(1,128)S(1)}, u32[]{:S(2)}, u32[]{:S(2)}) async-start(f32[128,1,128]{2,1,0:T(1,128)} %bitcast.24), calls=%async_computation.2 | async-start | bytes 131072 | tf_op jit(solution)/shard_map/all_to_all | solution.py:409
  54.5 0.7 collective-permute-done.1.low_ref
  55.2 0.0 collective-permute-done.2.high_ref
  55.2 0.0 copy-done.1
  55.2 7.7 %shard_map.72 = f32[6,4,32,256]{3,2,1,0:T(8,128)S(1)} custom-call(f32[6,4,32,256]{3,2,1,0:T(8,128)S(1)} %copy-done.1, f32[6,4,8,256]{3,2,1,0:T(8,128)S(1)} %collective-permute-done.edge_ref, f32[6,104,256]{2,1,0:T(8,128)S(1)} %collective-permute-done.1.low_ref, f32[6,104,256]{2,1,0:T(8,128)S(1)} %collective-permute-done.2.high_ref), custom_call_target="tpu_custom_call" | custom-call | flops 1 | bytes 1 | tf_op jit(solution)/shard_map/pallas_call | solution.py:480
  63.0 1.1 %all-to-all-done.2 = f32[128,1,128]{2,1,0:T(1,128)S(1)} async-done(((f32[128,1,128]{2,1,0:T(1,128)}), f32[128,1,128]{2,1,0:T(1,128)S(1)}, u32[]{:S(2)}, u32[]{:S(2)}) %all-to-all-start.2) | async-done | bytes 65568 | tf_op jit(solution)/shard_map/all_to_all | solution.py:409
  64.1 3.3 %shard_map.73 = f32[6,128,256]{2,1,0:T(8,128)} custom-call(s32[128,128]{1,0:T(8,128)S(1)} %bitcast.19, f32[128,128]{1,0:T(8,128)S(1)} %bitcast.20, f32[6,128,256]{2,1,0:T(8,128)S(1)} %bitcast.17), custom_call_target="tpu_custom_call" | custom-call | flops 1 | bytes 1 | tf_op jit(solution)/shard_map/pallas_call | solution.py:493
Async XLA Ops:
  3.6 11.7 %collective-permute-start = (f32[6,4,8,256]{3,2,1,0:T(8,128)S(1)}, f32[6,4,8,256]{3,2,1,0:T(8,128)S(1)}, u32[]{:S(2)}, u32[]{:S(2)}) collective-permute-start(f32[6,4,8,256]{3,2,1,0:T(8,128)S(1)} %constant_dynamic-slice_fusion), channel_id=1, source_target_pairs={{0,1},{1,0},{2,3},{3,2},{4,5},{5,4},{6,7},{7,6},{8,9},{9,8},{10,11... | collective-permute-start | bytes 589832 | tf_op jit(solution)/shard_map/ppermute | solution.py:462
  5.1 19.5 %all-to-all-start = ((s32[128,1,128]{2,1,0:T(1,128)}), s32[128,1,128]{2,1,0:T(1,128)S(1)}, u32[]{:S(2)}, u32[]{:S(2)}) async-start(s32[128,1,128]{2,1,0:T(1,128)} %bitcast.22), calls=%async_computation | async-start | bytes 131072 | tf_op jit(solution)/shard_map/all_to_all | solution.py:409
  15.3 1.1 %copy-start = (f32[6,4,32,256]{3,2,1,0:T(8,128)S(1)}, f32[6,4,32,256]{3,2,1,0:T(8,128)}, u32[]{:S(2)}) copy-start(f32[6,4,32,256]{3,2,1,0:T(8,128)} %gas_ref.3) | copy-start | bytes 2359300
  27.7 14.0 %all-to-all-start.1 = ((f32[128,1,128]{2,1,0:T(1,128)}), f32[128,1,128]{2,1,0:T(1,128)S(1)}, u32[]{:S(2)}, u32[]{:S(2)}) async-start(f32[128,1,128]{2,1,0:T(1,128)} %bitcast.7), calls=%async_computation.1 | async-start | bytes 131072 | tf_op jit(solution)/shard_map/all_to_all | solution.py:409
  32.4 22.9 %collective-permute-start.1 = (f32[6,104,256]{2,1,0:T(8,128)}, f32[6,104,256]{2,1,0:T(8,128)S(1)}, u32[]{:S(2)}, u32[]{:S(2)}) collective-permute-start(f32[6,104,256]{2,1,0:T(8,128)} %get-tuple-element.21), channel_id=1, source_target_pairs={{0,2},{2,4},{4,6},{6,8},{8,10},{10,12},{12,14},{14,16},{16,18},{18... | collective-permute-start | bytes 1916936 | tf_op jit(solution)/shard_map/ppermute | solution.py:473
  34.0 21.2 %collective-permute-start.2 = (f32[6,104,256]{2,1,0:T(8,128)S(1)}, f32[6,104,256]{2,1,0:T(8,128)S(1)}, u32[]{:S(2)}, u32[]{:S(2)}) collective-permute-start(f32[6,104,256]{2,1,0:T(8,128)S(1)} %get-tuple-element.22), channel_id=1, source_target_pairs={{2,0},{4,2},{6,4},{8,6},{10,8},{12,10},{14,12},{16,14},{18,16},{20... | collective-permute-start | bytes 1916936 | tf_op jit(solution)/shard_map/ppermute | solution.py:474
  41.8 0.6 copy-start.2
  42.4 12.8 %copy-start.1 = (f32[6,4,32,256]{3,2,1,0:T(8,128)S(1)}, f32[6,4,32,256]{3,2,1,0:T(8,128)}, u32[]{:S(2)}) copy-start(f32[6,4,32,256]{3,2,1,0:T(8,128)} %gas_ref.3) | copy-start | bytes 2359300
  49.9 14.2 %all-to-all-start.2 = ((f32[128,1,128]{2,1,0:T(1,128)}), f32[128,1,128]{2,1,0:T(1,128)S(1)}, u32[]{:S(2)}, u32[]{:S(2)}) async-start(f32[128,1,128]{2,1,0:T(1,128)} %bitcast.24), calls=%async_computation.2 | async-start | bytes 131072 | tf_op jit(solution)/shard_map/all_to_all | solution.py:409

commit v2 on v1

--- a/solution.py
+++ b/solution.py
@@ -15,7 +15,7 @@
 CHUNKS = BLK_DEV // LANES
 NSUB = 4
 NVAR = 5
-PIECES = 3
+PIECES = 2
 HALO = 3
 PART = 256
 PARCEL_FLOPS = 10**10
@@ -92,7 +92,7 @@
     req_ref[:, :CAP] = total.astype(jnp.int32) - 256
 
 
-def outward_kernel(gas_ref, edge_ref, table_ref, up_ref, down_ref):
+def table_kernel(gas_ref, table_ref):
     inverse = 1.0 / gas_ref[0].reshape(ROWS, NZ)
     for c in range(NVAR):
         value = gas_ref[1 + c].reshape(ROWS, NZ) * inverse
@@ -101,6 +101,9 @@
             for p, piece in enumerate(split(turned)):
                 start = p * 2 * ROWS + half * ROWS
                 table_ref[c * LANES : (c + 1) * LANES, start : start + ROWS] = piece
+
+
+def message_kernel(gas_ref, edge_ref, up_ref, down_ref):
     for i in range(HALO):
         here = slice(i * CY, (i + 1) * CY)
         up_ref[:, here, :] = gas_ref[:, CX - HALO + i]
@@ -168,11 +171,9 @@
 
 def parcel_kernel(
     owner_ref, rank_ref, live_ref, ans_ref, old_ref, new_ref, send_ref,
-    held, made, hot, turned, slots, alive, spread, placed, answered, got, sent, arrived,
+    held, made, hot, turned, slots, alive, spread, placed, outgoing, got, sent, posted,
 ):
     parts = BLK_DEV // PART
-    asking = pltpu.make_async_copy(ans_ref, answered, arrived)
-    asking.start()
     fetches = []
     for part in range(parts):
         here = slice(part * PART, (part + 1) * PART)
@@ -198,8 +199,7 @@
     shape = (PIECES * LANES, NVAR * LANES)
     spread[...] = ones_where((iota(shape, 0) % LANES) // CAP == iota(shape, 1) // LANES)
 
-    asking.wait()
-    answers = jnp.concatenate(split(answered[...]), axis=1)
+    answers = jnp.concatenate(split(ans_ref[...]), axis=1)
     kind = iota((PART, LANES), 1) // CAP
     stores = []
     for part in range(parts):
@@ -223,12 +223,15 @@
         for p, piece in enumerate(split(total)):
             placed[here, p * LANES : (p + 1) * LANES] = piece * slot
     send = dot(turned[...], placed[...])
-    send_ref[...] = sum(send[:, p * LANES : (p + 1) * LANES] for p in range(PIECES))
+    outgoing[...] = sum(send[:, p * LANES : (p + 1) * LANES] for p in range(PIECES))
+    post = pltpu.make_async_copy(outgoing, send_ref, posted)
+    post.start()
     for store in stores:
         store.wait()
-
-
-def scatter_kernel(asked_ref, come_ref, section_ref, out_ref, total):
+    post.wait()
+
+
+def scatter_kernel(asked_ref, come_ref, section_ref, out_ref, total, made, sent):
     row, lane = cell_parts(asked_ref)
     pieces = [p.astype(F32) for p in split(come_ref[...].T)]
     for pair in range(CAP // 2):
@@ -252,13 +255,24 @@
             total[...] = added
         else:
             total[...] += added
+    copies = []
+
+    def send(c):
+        copies.append(pltpu.make_async_copy(made.at[c], out_ref.at[c], sent.at[c]))
+        copies[-1].start()
+
     for c in range(NVAR):
         for half in range(2):
             cells = WEIGHT * total[c * LANES : (c + 1) * LANES, half * ROWS : (half + 1) * ROWS].T
             z = slice(half * LANES, (half + 1) * LANES)
-            out_ref[c, :, z] = section_ref[c, :, z] + cells
+            made[c, :, z] = section_ref[c, :, z] + cells
             if c == 0:
-                out_ref[NVAR, :, z] = section_ref[NVAR, :, z] + cells
+                made[NVAR, :, z] = section_ref[NVAR, :, z] + cells
+        send(c)
+        if c == 0:
+            send(NVAR)
+    for copy in copies:
+        copy.wait()
 
 
 def gas_kernel(gas_ref, edge_ref, low_ref, high_ref, out_ref, q0, q1, q2, prim, face):
@@ -291,31 +305,37 @@
         def _():
             q[:, HALO + CX] = q[:, HALO + CX - 1]
 
-    row_in_tile = iota((8, NZ), 0)
-    lane = iota((EXT_Y, LANES), 1)
-
-    def above(v, axis):
-        if axis == 0:
-            moved = pltpu.roll(v, EXT_Y - 1, 0)
-            tail = jnp.where(row_in_tile == 7, v[EXT_Y - 8 :], moved[EXT_Y - 8 :])
-            return jnp.concatenate([moved[: EXT_Y - 8], tail], axis=0)
-        left, right = v[:, :LANES], v[:, LANES:]
-        left_moved, right_moved = pltpu.roll(left, LANES - 1, 1), pltpu.roll(right, LANES - 1, 1)
-        at_end = lane == LANES - 1
-        return jnp.concatenate(
-            [jnp.where(at_end, right_moved, left_moved), jnp.where(at_end, right, right_moved)], axis=1
-        )
-
-    def below(g, first, axis):
-        if axis == 0:
-            moved = pltpu.roll(g, 1, 0)
-            head = jnp.where(row_in_tile == 0, first, moved[:8])
-            return jnp.concatenate([head, moved[8:]], axis=0)
-        left, right = pltpu.roll(g[:, :LANES], 1, 1), pltpu.roll(g[:, LANES:], 1, 1)
-        at_start = lane == 0
-        return jnp.concatenate(
-            [jnp.where(at_start, first, left), jnp.where(at_start, left, right)], axis=1
-        )
+    tiles, halves = EXT_Y // 8, range(NZ // LANES)
+    row_in_tile, lane = iota((8, LANES), 0), iota((8, LANES), 1)
+
+    def at(ref, c, x, t):
+        return [ref[c, x, 8 * t : 8 * t + 8, h * LANES : (h + 1) * LANES] for h in halves]
+
+    def each(f, *lists):
+        return [f(*items) for items in zip(*lists)]
+
+    def y_turned(v):
+        return [pltpu.roll(part, 7, 0) for part in v]
+
+    def y_above(v, turned, turned_next):
+        after = v if turned_next is None else turned_next
+        return each(lambda m, n: jnp.where(row_in_tile == 7, n, m), turned, after)
+
+    def z_above(v):
+        left, right = (pltpu.roll(part, LANES - 1, 1) for part in v)
+        return [jnp.where(lane == LANES - 1, right, left), jnp.where(lane == LANES - 1, v[1], right)]
+
+    def z_below(g, first):
+        left, right = (pltpu.roll(part, 1, 1) for part in g)
+        return [jnp.where(lane == 0, first, left), jnp.where(lane == 0, left, right)]
+
+    def weights(u, sound, un, soundn):
+        rate = each(lambda u, s, un, sn: jnp.maximum(jnp.abs(u) + s, jnp.abs(un) + sn), u, sound, un, soundn)
+        return each(jnp.add, u, rate), each(jnp.subtract, un, rate)
+
+    def face_flux(v, here, vn, there, p=None, pn=None):
+        g = each(lambda v, w, vn, wn: v * w + vn * wn, v, here, vn, there)
+        return g if p is None else each(lambda g, p, pn: g + (p + pn), g, p, pn)
 
     def primitives(q, x):
         inverse = 1.0 / q[0, x]
@@ -323,14 +343,12 @@
             prim[d, x] = q[1 + d, x] * inverse
         prim[3, x] = jnp.sqrt(GAMMA_ADIABATIC * (q[4, x] * inverse))
 
-    def x_faces(q, x):
-        u, un = prim[0, x], prim[0, x + 1]
-        rate = jnp.maximum(jnp.abs(u) + prim[3, x], jnp.abs(un) + prim[3, x + 1])
-        here, there = u + rate, un - rate
+    def x_faces(q, x, t):
+        here, there = weights(at(prim, 0, x, t), at(prim, 3, x, t), at(prim, 0, x + 1, t), at(prim, 3, x + 1, t))
         faces = []
         for c in range(6):
-            g = q[c, x] * here + q[c, x + 1] * there
-            faces.append(g + (q[4, x] + q[4, x + 1]) if c == 1 else g)
+            pressure = (at(q, 4, x, t), at(q, 4, x + 1, t)) if c == 1 else ()
+            faces.append(face_flux(at(q, c, x, t), here, at(q, c, x + 1, t), there, *pressure))
         return faces
 
     def update(q, combine, start, stop):
@@ -339,58 +357,94 @@
             return carry
 
         lax.fori_loop(start - 1, stop + 1, fill, 0)
-        for c, value in enumerate(x_faces(q, start - 1)):
-            face[c] = value
+        for t in range(tiles):
+            for c, value in enumerate(x_faces(q, start - 1, t)):
+                for h in halves:
+                    face[c, 8 * t : 8 * t + 8, h * LANES : (h + 1) * LANES] = value[h]
 
         def row(x, carry):
-            change = []
-            for c, upper in enumerate(x_faces(q, x)):
-                change.append(upper - face[c])
-                face[c] = upper
-            for axis in (0, 1):
-                d = 1 + axis
-                start_cells = (slice(0, 8), slice(None)) if axis == 0 else (slice(None), slice(0, LANES))
-                u = prim[d, x]
-                a = jnp.abs(u) + prim[3, x]
-                un = above(u, axis)
-                rate = jnp.maximum(a, above(a, axis))
-                here, there = u + rate, un - rate
+            turned = [y_turned(at(q, c, x, 0)) for c in range(6)]
+            turned_u, turned_s = y_turned(at(prim, 1, x, 0)), y_turned(at(prim, 3, x, 0))
+            shifted = [None] * 6
+            for t in range(tiles):
+                rows = slice(8 * t, 8 * t + 8)
+                final = t == tiles - 1
+                v = [at(q, c, x, t) for c in range(6)]
+                sound = at(prim, 3, x, t)
+
+                change = []
+                for c, upper in enumerate(x_faces(q, x, t)):
+                    z = [slice(h * LANES, (h + 1) * LANES) for h in halves]
+                    change.append([upper[h] - face[c, rows, z[h]] for h in halves])
+                    for h in halves:
+                        face[c, rows, z[h]] = upper[h]
+
+                u = at(prim, 1, x, t)
+                next_u = None if final else y_turned(at(prim, 1, x, t + 1))
+                next_s = None if final else y_turned(at(prim, 3, x, t + 1))
+                here, there = weights(u, sound, y_above(u, turned_u, next_u), y_above(sound, turned_s, next_s))
+                turned_u, turned_s = next_u, next_s
+                next_v = [None if final else y_turned(at(q, c, x, t + 1)) for c in range(6)]
+                above = [y_above(v[c], turned[c], next_v[c]) for c in range(6)]
+                turned = next_v
                 for c in range(6):
-                    v = q[c, x]
-                    g = v * here + above(v, axis) * there
-                    first = 2.0 * (v[start_cells] * u[start_cells])
-                    if c == 1 + d:
-                        p = q[4, x]
-                        g = g + (p + above(p, axis))
-                        first = first + 2.0 * p[start_cells]
-                    change[c] = change[c] + (g - below(g, first, axis))
-            for c in range(6):
-                combine(c, x, q[c, x] - (0.5 * LAM) * change[c])
+                    pressure = (v[4], above[4]) if c == 2 else ()
+                    g = face_flux(v[c], here, above[c], there, *pressure)
+                    moved = [pltpu.roll(part, 1, 0) for part in g]
+                    if t == 0:
+                        first = each(lambda v, u: 2.0 * (v * u), v[c], u)
+                        if c == 2:
+                            first = each(lambda f, p: f + 2.0 * p, first, v[4])
+                    else:
+                        first = shifted[c]
+                    below = each(lambda f, m: jnp.where(row_in_tile == 0, f, m), first, moved)
+                    shifted[c] = moved
+                    change[c] = each(lambda k, g, b: k + (g - b), change[c], g, below)
+
+                u = at(prim, 2, x, t)
+                here, there = weights(u, sound, z_above(u), z_above(sound))
+                above_p = z_above(v[4])
+                for c in range(6):
+                    above_v = above_p if c == 4 else z_above(v[c])
+                    pressure = (v[4], above_p) if c == 3 else ()
+                    g = face_flux(v[c], here, above_v, there, *pressure)
+                    first = 2.0 * (v[c][0] * u[0])
+                    if c == 3:
+                        first = first + 2.0 * v[4][0]
+                    below = z_below(g, first)
+                    change[c] = each(lambda k, g, b: k + (g - b), change[c], g, below)
+
+                for c in range(6):
+                    for h in halves:
+                        z = slice(h * LANES, (h + 1) * LANES)
+                        combine(c, x, rows, z, v[c][h] - (0.5 * LAM) * change[c][h])
             return carry
 
         lax.fori_loop(start, stop, row, 0)
 
     ghosts(q0)
 
-    def first_section(c, x, value):
-        q1[c, x] = value
+    def first_section(c, x, rows, z, value):
+        q1[c, x, rows, z] = value
 
     update(q0, first_section, 1, EXT_X - 1)
     ghosts(q1)
 
-    def second_section(c, x, value):
-        q2[c, x] = 0.75 * q0[c, x] + 0.25 * value
+    def second_section(c, x, rows, z, value):
+        q2[c, x, rows, z] = 0.75 * q0[c, x, rows, z] + 0.25 * value
 
     update(q1, second_section, 2, EXT_X - 2)
     ghosts(q2)
 
-    def third_section(c, x, value):
-        q1[c, x] = q0[c, x] * (1.0 / 3.0) + (2.0 / 3.0) * value
+    def third_section(c, x, rows, z, value):
+        q1[c, x, rows, z] = q0[c, x, rows, z] * (1.0 / 3.0) + (2.0 / 3.0) * value
 
     update(q2, third_section, HALO, HALO + CX)
     out_ref[...] = q1[:, inner, own, :]
 
 
+LARGE_FLOPS = 10**9
+LARGE = pl.CostEstimate(flops=LARGE_FLOPS, bytes_accessed=1, transcendentals=0)
 SMALL = pl.CostEstimate(flops=1, bytes_accessed=1, transcendentals=0)
 
 
@@ -409,12 +463,18 @@
     return lax.all_to_all(buffer, AXES, split_axis=0, concat_axis=0, tiled=True)
 
 
+HELD = pl.BlockSpec(memory_space=pltpu.VMEM)
+ANYWHERE = pl.BlockSpec(memory_space=pl.ANY)
+
+
+def in_hbm(array):
+    return pltpu.with_memory_space_constraint(array, pltpu.HBM)
+
+
 def integrate_parcels(owner, rank, live, answered, parcels):
-    held = pl.BlockSpec(memory_space=pltpu.VMEM)
-    far = pl.BlockSpec(memory_space=pl.ANY)
     return call(
         parcel_kernel,
-        60,
+        24,
         [
             jax.ShapeDtypeStruct((5, BLK_DEV, LANES), F32),
             jax.ShapeDtypeStruct((DEVICES, LANES), F32),
@@ -434,9 +494,9 @@
             pltpu.SemaphoreType.DMA,
         ],
         cost=pl.CostEstimate(flops=PARCEL_FLOPS, bytes_accessed=8 * 5 * BLK_DEV * LANES, transcendentals=0),
-        in_specs=[held, held, held, far, far],
-        out_specs=[far, held],
-    )(owner, rank, live, answered, parcels)
+        in_specs=[HELD] * 4 + [ANYWHERE],
+        out_specs=[ANYWHERE, ANYWHERE],
+    )(owner, rank, live, answered, in_hbm(parcels))
 
 
 def body(gas_state, particle_blocks, owner, host_cell, live_count):
@@ -449,27 +509,26 @@
 
     requests, rank = call(
         request_kernel,
-        60,
+        8,
         [
             jax.ShapeDtypeStruct((DEVICES, LANES), jnp.int32),
             jax.ShapeDtypeStruct((CHUNKS, LANES), jnp.int32),
         ],
-    )(owner, host_cell)
+    )(in_hbm(owner), in_hbm(host_cell))
     asked = deliver(requests)
 
     mine, _ = lax.optimization_barrier((gas_state, requests))
     edge = lax.dynamic_slice_in_dim(mine, (1 - pair) * (CY - 8), 8, axis=2)
     edge = lax.ppermute(edge, "grp", [(0, 1), (1, 0)])
+    table = call(
+        table_kernel, 12, jax.ShapeDtypeStruct((NVAR * LANES, PIECES * 2 * ROWS), BF16)
+    )(mine)
+    replies = call(gather_kernel, 16, square, [pltpu.VMEM((LANES, LANES), F32)], cost=LARGE)(asked, table)
+    answered = deliver(replies)
+
+    edge, replies = lax.optimization_barrier((edge, replies))
     message = jax.ShapeDtypeStruct((6, HALO * CY + 8, NZ), F32)
-    table, upward, downward = call(
-        outward_kernel,
-        12,
-        [jax.ShapeDtypeStruct((NVAR * LANES, PIECES * 2 * ROWS), BF16), message, message],
-    )(gas_state, edge)
-    replies = call(gather_kernel, 16, square, [pltpu.VMEM((LANES, LANES), F32)])(asked, table)
-    answered = deliver(replies)
-
-    upward, downward, _ = lax.optimization_barrier((upward, downward, replies))
+    upward, downward = call(message_kernel, 12, [message, message])(gas_state, edge)
     low = lax.ppermute(upward, "gas", [(i, (i + 1) % count) for i in range(count)])
     high = lax.ppermute(downward, "gas", [((i + 1) % count, i) for i in range(count)])
     parcels_next, sources = integrate_parcels(owner, rank, live, answered, particle_blocks)
@@ -494,7 +553,12 @@
         scatter_kernel,
         20,
         jax.ShapeDtypeStruct((6, ROWS, NZ), F32),
-        [pltpu.VMEM((NVAR * LANES, 2 * ROWS), F32)],
+        [
+            pltpu.VMEM((NVAR * LANES, 2 * ROWS), F32),
+            pltpu.VMEM((6, ROWS, NZ), F32),
+            pltpu.SemaphoreType.DMA((6,)),
+        ],
+        out_specs=ANYWHERE,
     )(asked, come, section_three.reshape(6, ROWS, NZ))
     return (gas_next.reshape(6, CX, CY, NZ), parcels_next)
 

time: 67.7 us -> 63.9 us (0.944)
  Pallas kernels: 24.8 us -> 20.8 us
  starting transfers between devices: 28.9 us -> 29.7 us
    ppermute x1, waiting for transfers between devices: 0.65 us -> 4.07 us  [body(): lax.ppermute(upward, 'gas', [(i, (i + 1) % count) for i in range(count)])]
    all_to_all x3, waiting for transfers between devices: 9.58 us -> 6.25 us  [deliver(): return lax.all_to_all(buffer, AXES, split_axis=0, concat_axis=0, tiled=True)]
    pallas_call x4 -> x5, Pallas kernels: 13.8 us -> 11.3 us  [the longest x1 5.38 us: integrate_parcels(): call(parcel_kernel, 24, [jax.ShapeDtypeStruct((5, BLK_DEV, LANES), F32),...]
    all_to_all x3, starting transfers between devices: 19.4 us -> 20.7 us  [deliver(): return lax.all_to_all(buffer, AXES, split_axis=0, concat_axis=0, tiled=True)]
    pallas_call x1, Pallas kernels: 7.75 us -> 6.97 us  [body(): call(gas_kernel, 28, jax.ShapeDtypeStruct((6, CX, CY, NZ), F32), [extende...]
    pallas_call x1, Pallas kernels: 3.26 us -> 2.5 us  [body(): call(scatter_kernel, 20, jax.ShapeDtypeStruct((6, ROWS, NZ), F32), [pltpu...]
    unnamed x6 -> x8, local copies, waits for them, and re-layouts: 1.75 us -> 1.15 us
  transfers between devices with their start and end apart: 6 -> 6, of which waited for: 4 -> 3; matrix products, arithmetic and copies ran while one was open for 0% -> 1% of each run, Pallas kernels for 24% -> 26%
where the time goes in v2:
time: 63.9 us; the launch traced here: 63.6 us
  starting transfers between devices  29.7 us (46%)
  Pallas kernels  20.8 us (33%)
  waiting for transfers between devices  10.3 us (16%)
  local copies, waits for them, and re-layouts  2.09 us (3%)
  between operations  0.73 us (1%)
    all_to_all x3, starting transfers between devices, deliver(): return lax.all_to_all(buffer, AXES, split_axis=0, concat_axis=0, tiled=True)  20.7 us
    pallas_call x1, Pallas kernels, body(): call(gas_kernel, 28, jax.ShapeDtypeStruct((6, CX, CY, NZ), F32), [extende...  6.97 us
    all_to_all x3, waiting for transfers between devices, deliver(): return lax.all_to_all(buffer, AXES, split_axis=0, concat_axis=0, tiled=True)  6.25 us
    ppermute x1, starting transfers between devices, body(): lax.ppermute(downward, 'gas', [((i + 1) % count, i) for i in range(count)])  6.22 us
    pallas_call x1, Pallas kernels, integrate_parcels(): call(parcel_kernel, 24, [jax.ShapeDtypeStruct((5, BLK_DEV, LANES), F32),...  5.38 us
    ppermute x1, waiting for transfers between devices, body(): lax.ppermute(upward, 'gas', [(i, (i + 1) % count) for i in range(count)])  4.07 us
    pallas_call x1, Pallas kernels, body(): call(gather_kernel, 16, square, [pltpu.VMEM((LANES, LANES), F32)], cost=L...  2.5 us
    pallas_call x1, Pallas kernels, body(): call(scatter_kernel, 20, jax.ShapeDtypeStruct((6, ROWS, NZ), F32), [pltpu...  2.5 us
  transfers between devices with their start and end apart: 6, of which 3 were waited for; matrix products, arithmetic and copies ran while one was open for 1% of the time, Pallas kernels for 26%

profile of v2, /device:TPU:1, one launch (start us, length us, event | category | flops | bytes accessed | tf_op | source)
XLA Modules:
  0.0 63.6 jit_solution(12018073073857965075)
XLA Ops:
  0.6 2.0 %shard_map.68 = (s32[128,128]{1,0:T(8,128)}, s32[8,128]{1,0:T(8,128)S(1)}) custom-call(s32[8,128]{1,0:T(8,128)} %bitcast.22, s32[8,128]{1,0:T(8,128)} %bitcast.26), custom_call_target="tpu_custom_call" | custom-call | flops 1 | bytes 1 | tf_op jit(solution)/shard_map/pallas_call | solution.py:510
  2.7 11.5 %all-to-all-start = ((s32[128,1,128]{2,1,0:T(1,128)}), s32[128,1,128]{2,1,0:T(1,128)S(1)}, u32[]{:S(2)}, u32[]{:S(2)}) async-start(s32[128,1,128]{2,1,0:T(1,128)} %bitcast.3), calls=%async_computation | async-start | bytes 131072 | tf_op jit(solution)/shard_map/all_to_all | solution.py:463
  14.2 0.9 %constant_dynamic-slice_fusion = f32[6,4,8,256]{3,2,1,0:T(8,128)S(1)} fusion(f32[6,4,32,256]{3,2,1,0:T(8,128)} %gas_ref.4, s32[]{:T(128)S(6)} %select_n.3), kind=kLoop, calls=%fused_computation | loop fusion | bytes 393220 | tf_op jit(solution)/shard_map/dynamic_slice | solution.py:521
  15.1 1.1 %collective-permute-start = (f32[6,4,8,256]{3,2,1,0:T(8,128)S(1)}, f32[6,4,8,256]{3,2,1,0:T(8,128)S(1)}, u32[]{:S(2)}, u32[]{:S(2)}) collective-permute-start(f32[6,4,8,256]{3,2,1,0:T(8,128)S(1)} %constant_dynamic-slice_fusion), channel_id=1, source_target_pairs={{0,1},{1,0},{2,3},{3,2},{4,5},{5,4},{6,7},{7,6},{8,9},{9,8},{10,11... | collective-permute-start | bytes 589832 | tf_op jit(solution)/shard_map/ppermute | solution.py:522
  16.3 0.0 copy-start
  16.3 1.1 %copy-done = f32[6,4,32,256]{3,2,1,0:T(8,128)S(1)} copy-done((f32[6,4,32,256]{3,2,1,0:T(8,128)S(1)}, f32[6,4,32,256]{3,2,1,0:T(8,128)}, u32[]{:S(2)}) %copy-start) | copy-done | bytes 786456
  17.4 0.0 copy-start.1
  17.4 0.2 shard_map.69.table_ref
  17.7 0.0 copy-start.2
  17.7 0.0 copy-start.3
  17.7 5.8 %all-to-all-done = s32[128,1,128]{2,1,0:T(1,128)S(1)} async-done(((s32[128,1,128]{2,1,0:T(1,128)}), s32[128,1,128]{2,1,0:T(1,128)S(1)}, u32[]{:S(2)}, u32[]{:S(2)}) %all-to-all-start) | async-done | bytes 65568 | tf_op jit(solution)/shard_map/all_to_all | solution.py:463
  23.5 2.5 %shard_map.70 = f32[128,128]{1,0:T(8,128)} custom-call(s32[128,128]{1,0:T(8,128)S(1)} %bitcast.18, bf16[640,512]{1,0:T(8,128)(2,1)S(1)} %shard_map.69.table_ref), custom_call_target="tpu_custom_call" | custom-call | flops 1000000000 | bytes 1 | tf_op jit(solution)/shard_map/pallas_call | solution.py:526
  26.0 4.6 %all-to-all-start.1 = ((f32[128,1,128]{2,1,0:T(1,128)}), f32[128,1,128]{2,1,0:T(1,128)S(1)}, u32[]{:S(2)}, u32[]{:S(2)}) async-start(f32[128,1,128]{2,1,0:T(1,128)} %bitcast.7), calls=%async_computation.1 | async-start | bytes 131072 | tf_op jit(solution)/shard_map/all_to_all | solution.py:463
  30.6 0.0 collective-permute-done.edge_ref
  30.6 0.0 copy-done.1
  30.6 1.2 %shard_map.72 = (f32[6,104,256]{2,1,0:T(8,128)}, f32[6,104,256]{2,1,0:T(8,128)}) custom-call(f32[6,4,32,256]{3,2,1,0:T(8,128)S(1)} %copy-done.1, f32[6,4,8,256]{3,2,1,0:T(8,128)S(1)} %collective-permute-done.edge_ref), custom_call_target="tpu_custom_call" | custom-call | flops 1 | bytes 1 | tf_op jit(solution)/shard_map/pallas_call | solution.py:531
  31.8 1.6 %collective-permute-start.1 = (f32[6,104,256]{2,1,0:T(8,128)}, f32[6,104,256]{2,1,0:T(8,128)S(1)}, u32[]{:S(2)}, u32[]{:S(2)}) collective-permute-start(f32[6,104,256]{2,1,0:T(8,128)} %get-tuple-element.17), channel_id=1, source_target_pairs={{0,2},{2,4},{4,6},{6,8},{8,10},{10,12},{12,14},{14,16},{16,18},{18... | collective-permute-start | bytes 1916936 | tf_op jit(solution)/shard_map/ppermute | solution.py:532
  33.4 6.2 %collective-permute-start.2 = (f32[6,104,256]{2,1,0:T(8,128)}, f32[6,104,256]{2,1,0:T(8,128)S(1)}, u32[]{:S(2)}, u32[]{:S(2)}) collective-permute-start(f32[6,104,256]{2,1,0:T(8,128)} %get-tuple-element.18), channel_id=1, source_target_pairs={{2,0},{4,2},{6,4},{8,6},{10,8},{12,10},{14,12},{16,14},{18,16},{20... | collective-permute-start | bytes 1916936 | tf_op jit(solution)/shard_map/ppermute | solution.py:533
  39.6 0.4 all-to-all-done.1
  40.0 0.0 copy-done.2
  40.0 0.0 copy-done.3
  40.1 5.4 %shard_map.71 = (f32[5,1024,128]{2,1,0:T(8,128)}, f32[128,128]{1,0:T(8,128)}) custom-call(s32[8,128]{1,0:T(8,128)S(1)} %bitcast.23, s32[8,128]{1,0:T(8,128)S(1)} %get-tuple-element.13.rank_ref, s32[8,128]{1,0:T(8,128)S(1)} %bitcast.24, f32[128,128]{1,0:T(8,128)S(1)} %bitcast.21, f32[5,1024,128]{2,1,0:T(8,128)} %old_ref.1), custom_call_target="tpu_custom_call" | custom-call | flops 10000000000 | bytes 5242880 | tf_op jit(solution)/shard_map/pallas_call | solution.py:475
  45.4 4.6 %all-to-all-start.2 = ((f32[128,1,128]{2,1,0:T(1,128)}), f32[128,1,128]{2,1,0:T(1,128)S(1)}, u32[]{:S(2)}, u32[]{:S(2)}) async-start(f32[128,1,128]{2,1,0:T(1,128)} %bitcast.10), calls=%async_computation.2 | async-start | bytes 131072 | tf_op jit(solution)/shard_map/all_to_all | solution.py:463
  50.0 4.1 %collective-permute-done.1.low_ref = f32[6,104,256]{2,1,0:T(8,128)S(1)} collective-permute-done((f32[6,104,256]{2,1,0:T(8,128)}, f32[6,104,256]{2,1,0:T(8,128)S(1)}, u32[]{:S(2)}, u32[]{:S(2)}) %collective-permute-start.1) | collective-permute-done | bytes 639008 | tf_op jit(solution)/shard_map/ppermute | solution.py:532
  54.1 0.0 collective-permute-done.2.high_ref
  54.1 7.0 %shard_map.73 = f32[6,4,32,256]{3,2,1,0:T(8,128)S(1)} custom-call(f32[6,4,32,256]{3,2,1,0:T(8,128)S(1)} %copy-done.1, f32[6,4,8,256]{3,2,1,0:T(8,128)S(1)} %collective-permute-done.edge_ref, f32[6,104,256]{2,1,0:T(8,128)S(1)} %collective-permute-done.1.low_ref, f32[6,104,256]{2,1,0:T(8,128)S(1)} %collective-permute-done.2.high_ref), custom_call_target="tpu_custom_call" | custom-call | flops 1 | bytes 1 | tf_op jit(solution)/shard_map/pallas_call | solution.py:539
  61.1 0.0 all-to-all-done.2
  61.1 2.5 %shard_map.74 = f32[6,128,256]{2,1,0:T(8,128)} custom-call(s32[128,128]{1,0:T(8,128)S(1)} %bitcast.19, f32[128,128]{1,0:T(8,128)S(1)} %bitcast.20, f32[6,128,256]{2,1,0:T(8,128)S(1)} %bitcast.17), custom_call_target="tpu_custom_call" | custom-call | flops 1 | bytes 1 | tf_op jit(solution)/shard_map/pallas_call | solution.py:552
Async XLA Ops:
  2.7 20.8 %all-to-all-start = ((s32[128,1,128]{2,1,0:T(1,128)}), s32[128,1,128]{2,1,0:T(1,128)S(1)}, u32[]{:S(2)}, u32[]{:S(2)}) async-start(s32[128,1,128]{2,1,0:T(1,128)} %bitcast.3), calls=%async_computation | async-start | bytes 131072 | tf_op jit(solution)/shard_map/all_to_all | solution.py:463
  15.1 15.5 %collective-permute-start = (f32[6,4,8,256]{3,2,1,0:T(8,128)S(1)}, f32[6,4,8,256]{3,2,1,0:T(8,128)S(1)}, u32[]{:S(2)}, u32[]{:S(2)}) collective-permute-start(f32[6,4,8,256]{3,2,1,0:T(8,128)S(1)} %constant_dynamic-slice_fusion), channel_id=1, source_target_pairs={{0,1},{1,0},{2,3},{3,2},{4,5},{5,4},{6,7},{7,6},{8,9},{9,8},{10,11... | collective-permute-start | bytes 589832 | tf_op jit(solution)/shard_map/ppermute | solution.py:522
  16.3 1.1 %copy-start = (f32[6,4,32,256]{3,2,1,0:T(8,128)S(1)}, f32[6,4,32,256]{3,2,1,0:T(8,128)}, u32[]{:S(2)}) copy-start(f32[6,4,32,256]{3,2,1,0:T(8,128)} %gas_ref.4) | copy-start | bytes 2359300
  17.4 13.2 %copy-start.1 = (f32[6,4,32,256]{3,2,1,0:T(8,128)S(1)}, f32[6,4,32,256]{3,2,1,0:T(8,128)}, u32[]{:S(2)}) copy-start(f32[6,4,32,256]{3,2,1,0:T(8,128)} %gas_ref.4) | copy-start | bytes 2359300
  17.7 22.4 %copy-start.2 = (s32[1024,1]{0,1:T(1,128)S(1)}, s32[1024,1]{0,1:T(1,128)}, u32[]{:S(2)}) copy-start(s32[1024,1]{0,1:T(1,128)} %param.7) | copy-start | bytes 12292
  17.7 22.4 %copy-start.3 = (s32[1024]{0:T(1024)S(1)}, s32[1024]{0:T(1024)}, u32[]{:S(2)}) copy-start(s32[1024]{0:T(1024)} %param.9) | copy-start | bytes 12292
  26.0 14.0 %all-to-all-start.1 = ((f32[128,1,128]{2,1,0:T(1,128)}), f32[128,1,128]{2,1,0:T(1,128)S(1)}, u32[]{:S(2)}, u32[]{:S(2)}) async-start(f32[128,1,128]{2,1,0:T(1,128)} %bitcast.7), calls=%async_computation.1 | async-start | bytes 131072 | tf_op jit(solution)/shard_map/all_to_all | solution.py:463
  31.8 22.3 %collective-permute-start.1 = (f32[6,104,256]{2,1,0:T(8,128)}, f32[6,104,256]{2,1,0:T(8,128)S(1)}, u32[]{:S(2)}, u32[]{:S(2)}) collective-permute-start(f32[6,104,256]{2,1,0:T(8,128)} %get-tuple-element.17), channel_id=1, source_target_pairs={{0,2},{2,4},{4,6},{6,8},{8,10},{10,12},{12,14},{14,16},{16,18},{18... | collective-permute-start | bytes 1916936 | tf_op jit(solution)/shard_map/ppermute | solution.py:532
  33.4 20.7 %collective-permute-start.2 = (f32[6,104,256]{2,1,0:T(8,128)}, f32[6,104,256]{2,1,0:T(8,128)S(1)}, u32[]{:S(2)}, u32[]{:S(2)}) collective-permute-start(f32[6,104,256]{2,1,0:T(8,128)} %get-tuple-element.18), channel_id=1, source_target_pairs={{2,0},{4,2},{6,4},{8,6},{10,8},{12,10},{14,12},{16,14},{18,16},{20... | collective-permute-start | bytes 1916936 | tf_op jit(solution)/shard_map/ppermute | solution.py:533
  45.4 15.7 %all-to-all-start.2 = ((f32[128,1,128]{2,1,0:T(1,128)}), f32[128,1,128]{2,1,0:T(1,128)S(1)}, u32[]{:S(2)}, u32[]{:S(2)}) async-start(f32[128,1,128]{2,1,0:T(1,128)} %bitcast.10), calls=%async_computation.2 | async-start | bytes 131072 | tf_op jit(solution)/shard_map/all_to_all | solution.py:463

commit v3 on v2

--- a/solution.py
+++ b/solution.py
@@ -17,6 +17,7 @@
 NVAR = 5
 PIECES = 2
 HALO = 3
+FAR = HALO - 1
 PART = 256
 PARCEL_FLOPS = 10**10
 EXT_X = CX + 2 * HALO
@@ -92,7 +93,18 @@
     req_ref[:, :CAP] = total.astype(jnp.int32) - 256
 
 
-def table_kernel(gas_ref, table_ref):
+def by_core(action, *refs):
+    pair = lax.axis_index("grp")
+    for core in range(2):
+        pl.when(pair == core)(lambda: action(core, *refs))
+
+
+def table_kernel(gas_ref, table_ref, first_ref, second_ref):
+    def outermost(pair, up_ref, down_ref):
+        up_ref[...] = gas_ref[:, CX - 1]
+        down_ref[...] = gas_ref[:, 0]
+
+    by_core(outermost, first_ref, second_ref)
     inverse = 1.0 / gas_ref[0].reshape(ROWS, NZ)
     for c in range(NVAR):
         value = gas_ref[1 + c].reshape(ROWS, NZ) * inverse
@@ -103,23 +115,22 @@
                 table_ref[c * LANES : (c + 1) * LANES, start : start + ROWS] = piece
 
 
-def message_kernel(gas_ref, edge_ref, up_ref, down_ref):
-    for i in range(HALO):
-        here = slice(i * CY, (i + 1) * CY)
-        up_ref[:, here, :] = gas_ref[:, CX - HALO + i]
-        down_ref[:, here, :] = gas_ref[:, i]
-    at = HALO * CY
-
-    def corners(near, after):
+def message_kernel(gas_ref, edge_ref, first_ref, second_ref):
+    at = FAR * CY
+
+    def fill(pair, up_ref, down_ref):
+        near, after = ((0, 1), (7, 6))[pair]
+        for i in range(FAR):
+            here = slice(i * CY, (i + 1) * CY)
+            up_ref[:, here, :] = gas_ref[:, CX - HALO + i]
+            down_ref[:, here, :] = gas_ref[:, 1 + i]
         for ref, one, two in ((up_ref, CX - 1, CX - 2), (down_ref, 0, 1)):
             ref[:, at : at + 8, :] = jnp.zeros((6, 8, NZ), F32)
             ref[:, at : at + 1, :] = edge_ref[:, one, near : near + 1, :]
             ref[:, at + 1 : at + 2, :] = edge_ref[:, one, after : after + 1, :]
             ref[:, at + 2 : at + 3, :] = edge_ref[:, two, near : near + 1, :]
 
-    pair = lax.axis_index("grp")
-    pl.when(pair == 0)(lambda: corners(0, 1))
-    pl.when(pair == 1)(lambda: corners(7, 6))
+    by_core(fill, first_ref, second_ref)
 
 
 def cell_parts(asked_ref):
@@ -275,26 +286,33 @@
         copy.wait()
 
 
-def gas_kernel(gas_ref, edge_ref, low_ref, high_ref, out_ref, q0, q1, q2, prim, face):
+def gas_kernel(gas_ref, edge_ref, below, above, low, high, out_ref, q0, q1, q2, prim, face):
     place, pair = lax.axis_index("gas"), lax.axis_index("grp")
     own = pl.ds(pl.multiple_of(pair * 8, 8), CY)
     side = pl.ds(pl.multiple_of((1 - pair) * CY, 8), 8)
     inner = slice(HALO, HALO + CX)
     q0[:, inner, own, :] = gas_ref[...]
     q0[:, inner, side, :] = edge_ref[...]
-    for i in range(HALO):
-        q0[:, i, own, :] = low_ref[:, i * CY : (i + 1) * CY, :]
-        q0[:, HALO + CX + i, own, :] = high_ref[:, i * CY : (i + 1) * CY, :]
-
-    def corners(near, after):
-        at = HALO * CY
+    at_corner = FAR * CY
+
+    def rows_beside(pair, below_ref, above_ref):
+        mine = slice(8 * pair, 8 * pair + CY)
+        q0[:, HALO - 1, mine, :] = below_ref[...]
+        q0[:, HALO + CX, mine, :] = above_ref[...]
+
+    def rows_beyond(pair, low_ref, high_ref):
+        mine = slice(8 * pair, 8 * pair + CY)
+        near, after = ((CY, CY + 1), (7, 6))[pair]
+        for i in range(FAR):
+            q0[:, i, mine, :] = low_ref[:, i * CY : (i + 1) * CY, :]
+            q0[:, HALO + CX + 1 + i, mine, :] = high_ref[:, i * CY : (i + 1) * CY, :]
         for ref, one, two in ((low_ref, HALO - 1, HALO - 2), (high_ref, HALO + CX, HALO + CX + 1)):
-            q0[:, one, near : near + 1, :] = ref[:, at : at + 1, :]
-            q0[:, one, after : after + 1, :] = ref[:, at + 1 : at + 2, :]
-            q0[:, two, near : near + 1, :] = ref[:, at + 2 : at + 3, :]
-
-    pl.when(pair == 0)(lambda: corners(CY, CY + 1))
-    pl.when(pair == 1)(lambda: corners(7, 6))
+            q0[:, one, near : near + 1, :] = ref[:, at_corner : at_corner + 1, :]
+            q0[:, one, after : after + 1, :] = ref[:, at_corner + 1 : at_corner + 2, :]
+            q0[:, two, near : near + 1, :] = ref[:, at_corner + 2 : at_corner + 3, :]
+
+    by_core(rows_beside, below, above)
+    by_core(rows_beyond, low, high)
 
     def ghosts(q):
         @pl.when(place == 0)
@@ -356,7 +374,7 @@
             primitives(q, x)
             return carry
 
-        lax.fori_loop(start - 1, stop + 1, fill, 0)
+        lax.fori_loop(start - 1, stop + 1, fill, 0, unroll=2)
         for t in range(tiles):
             for c, value in enumerate(x_faces(q, start - 1, t)):
                 for h in halves:
@@ -520,21 +538,30 @@
     mine, _ = lax.optimization_barrier((gas_state, requests))
     edge = lax.dynamic_slice_in_dim(mine, (1 - pair) * (CY - 8), 8, axis=2)
     edge = lax.ppermute(edge, "grp", [(0, 1), (1, 0)])
-    table = call(
-        table_kernel, 12, jax.ShapeDtypeStruct((NVAR * LANES, PIECES * 2 * ROWS), BF16)
+    circuit = [(i, (i + 1) % count) for i in range(count)]
+    back = [(target, source) for source, target in circuit]
+    row = jax.ShapeDtypeStruct((6, CY, NZ), F32)
+    table, first, second = call(
+        table_kernel, 12, [jax.ShapeDtypeStruct((NVAR * LANES, PIECES * 2 * ROWS), BF16), row, row]
     )(mine)
+    below = lax.ppermute(first, "gas", circuit)
+    above = lax.ppermute(second, "gas", back)
     replies = call(gather_kernel, 16, square, [pltpu.VMEM((LANES, LANES), F32)], cost=LARGE)(asked, table)
     answered = deliver(replies)
 
-    edge, replies = lax.optimization_barrier((edge, replies))
-    message = jax.ShapeDtypeStruct((6, HALO * CY + 8, NZ), F32)
-    upward, downward = call(message_kernel, 12, [message, message])(gas_state, edge)
-    low = lax.ppermute(upward, "gas", [(i, (i + 1) % count) for i in range(count)])
-    high = lax.ppermute(downward, "gas", [((i + 1) % count, i) for i in range(count)])
+    edge, below, above, replies = lax.optimization_barrier(
+        (edge, below, above, replies)
+    )
+    message = jax.ShapeDtypeStruct((6, FAR * CY + 8, NZ), F32)
+    first, second = call(message_kernel, 12, [message, message])(gas_state, edge)
+    low = lax.ppermute(first, "gas", circuit)
+    high = lax.ppermute(second, "gas", back)
     parcels_next, sources = integrate_parcels(owner, rank, live, answered, particle_blocks)
     come = deliver(sources)
 
-    low, high, _ = lax.optimization_barrier((low, high, sources))
+    below, above, low, high, _ = lax.optimization_barrier(
+        (below, above, low, high, sources)
+    )
     extended = pltpu.VMEM((6, EXT_X, EXT_Y, NZ), F32)
     section_three = call(
         gas_kernel,
@@ -547,7 +574,7 @@
             pltpu.VMEM((4, EXT_X, EXT_Y, NZ), F32),
             pltpu.VMEM((6, EXT_Y, NZ), F32),
         ],
-    )(gas_state, edge, low, high)
+    )(gas_state, edge, below, above, low, high)
 
     gas_next = call(
         scatter_kernel,

time: 63.9 us -> 63.1 us (0.987)
  waiting for transfers between devices: 10.3 us -> 3.41 us
  starting transfers between devices: 29.7 us -> 36.1 us
    ppermute x2 -> x4, starting transfers between devices: 7.82 us -> 15 us  [the longest x1 6.3 us: body(): above = lax.ppermute(second, 'gas', back)]
    ppermute x2 -> x4, waiting for transfers between devices: 4.07 us -> 0.01 us  [the longest x1 0.01 us: body(): below = lax.ppermute(first, 'gas', circuit)]
    all_to_all x3, waiting for transfers between devices: 6.25 us -> 3.39 us  [deliver(): return lax.all_to_all(buffer, AXES, split_axis=0, concat_axis=0, tiled=True)]
    all_to_all x3, starting transfers between devices: 20.7 us -> 19.9 us  [deliver(): return lax.all_to_all(buffer, AXES, split_axis=0, concat_axis=0, tiled=True)]
  transfers between devices with their start and end apart: 6 -> 8, of which waited for: 3 -> 2; matrix products, arithmetic and copies ran while one was open for 1% -> 2% of each run, Pallas kernels for 26% -> 25%
where the time goes in v3:
time: 63.1 us; the launch traced here: 62.8 us
  starting transfers between devices  36.1 us (57%)
  Pallas kernels  20.4 us (32%)
  waiting for transfers between devices  3.41 us (5%)
  local copies, waits for them, and re-layouts  2.09 us (3%)
  between operations  0.74 us (1%)
    all_to_all x3, starting transfers between devices, deliver(): return lax.all_to_all(buffer, AXES, split_axis=0, concat_axis=0, tiled=True)  19.9 us
    pallas_call x1, Pallas kernels, body(): call(gas_kernel, 28, jax.ShapeDtypeStruct((6, CX, CY, NZ), F32), [extende...  6.83 us
    ppermute x1, starting transfers between devices, body(): above = lax.ppermute(second, 'gas', back)  6.3 us
    ppermute x1, starting transfers between devices, body(): high = lax.ppermute(second, 'gas', back)  6.22 us
    pallas_call x1, Pallas kernels, integrate_parcels(): call(parcel_kernel, 24, [jax.ShapeDtypeStruct((5, BLK_DEV, LANES), F32),...  5.4 us
    all_to_all x3, waiting for transfers between devices, deliver(): return lax.all_to_all(buffer, AXES, split_axis=0, concat_axis=0, tiled=True)  3.39 us
    pallas_call x1, Pallas kernels, body(): call(gather_kernel, 16, square, [pltpu.VMEM((LANES, LANES), F32)], cost=L...  2.53 us
    pallas_call x1, Pallas kernels, body(): call(scatter_kernel, 20, jax.ShapeDtypeStruct((6, ROWS, NZ), F32), [pltpu...  2.49 us
  transfers between devices with their start and end apart: 8, of which 2 were waited for; matrix products, arithmetic and copies ran while one was open for 2% of the time, Pallas kernels for 25%

profile of v3, /device:TPU:1, one launch (start us, length us, event | category | flops | bytes accessed | tf_op | source)
XLA Modules:
  0.0 62.8 jit_solution(15613891388499942107)
XLA Ops:
  0.6 2.0 %shard_map.68 = (s32[128,128]{1,0:T(8,128)}, s32[8,128]{1,0:T(8,128)S(1)}) custom-call(s32[8,128]{1,0:T(8,128)} %bitcast.22, s32[8,128]{1,0:T(8,128)} %bitcast.26), custom_call_target="tpu_custom_call" | custom-call | flops 1 | bytes 1 | tf_op jit(solution)/shard_map/pallas_call | solution.py:528
  2.7 11.5 %all-to-all-start = ((s32[128,1,128]{2,1,0:T(1,128)}), s32[128,1,128]{2,1,0:T(1,128)S(1)}, u32[]{:S(2)}, u32[]{:S(2)}) async-start(s32[128,1,128]{2,1,0:T(1,128)} %bitcast.3), calls=%async_computation | async-start | bytes 131072 | tf_op jit(solution)/shard_map/all_to_all | solution.py:481
  14.2 0.9 %constant_dynamic-slice_fusion = f32[6,4,8,256]{3,2,1,0:T(8,128)S(1)} fusion(f32[6,4,32,256]{3,2,1,0:T(8,128)} %gas_ref.4, s32[]{:T(128)S(6)} %select_n.3), kind=kLoop, calls=%fused_computation | loop fusion | bytes 393220 | tf_op jit(solution)/shard_map/dynamic_slice | solution.py:539
  15.1 1.1 %collective-permute-start = (f32[6,4,8,256]{3,2,1,0:T(8,128)S(1)}, f32[6,4,8,256]{3,2,1,0:T(8,128)S(1)}, u32[]{:S(2)}, u32[]{:S(2)}) collective-permute-start(f32[6,4,8,256]{3,2,1,0:T(8,128)S(1)} %constant_dynamic-slice_fusion), channel_id=1, source_target_pairs={{0,1},{1,0},{2,3},{3,2},{4,5},{5,4},{6,7},{7,6},{8,9},{9,8},{10,11... | collective-permute-start | bytes 589832 | tf_op jit(solution)/shard_map/ppermute | solution.py:540
  16.3 0.0 copy-start
  16.3 1.1 %copy-done = f32[6,4,32,256]{3,2,1,0:T(8,128)S(1)} copy-done((f32[6,4,32,256]{3,2,1,0:T(8,128)S(1)}, f32[6,4,32,256]{3,2,1,0:T(8,128)}, u32[]{:S(2)}) %copy-start) | copy-done | bytes 786456
  17.4 0.0 copy-start.1
  17.4 0.0 copy-start.2
  17.4 0.0 copy-start.3
  17.4 0.3 shard_map.69
  17.7 0.9 %collective-permute-start.1 = (f32[6,32,256]{2,1,0:T(8,128)S(1)}, f32[6,32,256]{2,1,0:T(8,128)S(1)}, u32[]{:S(2)}, u32[]{:S(2)}) collective-permute-start(f32[6,32,256]{2,1,0:T(8,128)S(1)} %get-tuple-element.24), channel_id=1, source_target_pairs={{0,2},{2,4},{4,6},{6,8},{8,10},{10,12},{12,14},{14,16},{16,18},{18... | collective-permute-start | bytes 589832 | tf_op jit(solution)/shard_map/ppermute | solution.py:547
  18.6 6.3 %collective-permute-start.2 = (f32[6,32,256]{2,1,0:T(8,128)S(1)}, f32[6,32,256]{2,1,0:T(8,128)S(1)}, u32[]{:S(2)}, u32[]{:S(2)}) collective-permute-start(f32[6,32,256]{2,1,0:T(8,128)S(1)} %get-tuple-element.25), channel_id=1, source_target_pairs={{2,0},{4,2},{6,4},{8,6},{10,8},{12,10},{14,12},{16,14},{18,16},{20... | collective-permute-start | bytes 589832 | tf_op jit(solution)/shard_map/ppermute | solution.py:548
  24.9 0.0 all-to-all-done
  24.9 2.5 %shard_map.70 = f32[128,128]{1,0:T(8,128)} custom-call(s32[128,128]{1,0:T(8,128)S(1)} %bitcast.18, bf16[640,512]{1,0:T(8,128)(2,1)S(1)} %get-tuple-element.22.table_ref), custom_call_target="tpu_custom_call" | custom-call | flops 1000000000 | bytes 1 | tf_op jit(solution)/shard_map/pallas_call | solution.py:549
  27.4 3.8 %all-to-all-start.1 = ((f32[128,1,128]{2,1,0:T(1,128)}), f32[128,1,128]{2,1,0:T(1,128)S(1)}, u32[]{:S(2)}, u32[]{:S(2)}) async-start(f32[128,1,128]{2,1,0:T(1,128)} %bitcast.7), calls=%async_computation.1 | async-start | bytes 131072 | tf_op jit(solution)/shard_map/all_to_all | solution.py:481
  31.2 0.0 collective-permute-done.edge_ref
  31.3 0.0 collective-permute-done.1.below
  31.3 0.0 collective-permute-done.2.above
  31.3 0.0 copy-done.1
  31.3 0.8 %shard_map.72 = (f32[6,72,256]{2,1,0:T(8,128)}, f32[6,72,256]{2,1,0:T(8,128)S(1)}) custom-call(f32[6,4,32,256]{3,2,1,0:T(8,128)S(1)} %copy-done.1, f32[6,4,8,256]{3,2,1,0:T(8,128)S(1)} %collective-permute-done.edge_ref), custom_call_target="tpu_custom_call" | custom-call | flops 1 | bytes 1 | tf_op jit(solution)/shard_map/pallas_call | solution.py:556
  32.1 1.6 %collective-permute-start.3 = (f32[6,72,256]{2,1,0:T(8,128)}, f32[6,72,256]{2,1,0:T(8,128)S(1)}, u32[]{:S(2)}, u32[]{:S(2)}) collective-permute-start(f32[6,72,256]{2,1,0:T(8,128)} %get-tuple-element.29), channel_id=1, source_target_pairs={{0,2},{2,4},{4,6},{6,8},{8,10},{10,12},{12,14},{14,16},{16,18},{18... | collective-permute-start | bytes 1327112 | tf_op jit(solution)/shard_map/ppermute | solution.py:557
  33.8 6.2 %collective-permute-start.4 = (f32[6,72,256]{2,1,0:T(8,128)S(1)}, f32[6,72,256]{2,1,0:T(8,128)S(1)}, u32[]{:S(2)}, u32[]{:S(2)}) collective-permute-start(f32[6,72,256]{2,1,0:T(8,128)S(1)} %get-tuple-element.30), channel_id=1, source_target_pairs={{2,0},{4,2},{6,4},{8,6},{10,8},{12,10},{14,12},{16,14},{18,16},{20... | collective-permute-start | bytes 1327112 | tf_op jit(solution)/shard_map/ppermute | solution.py:558
  40.0 0.7 %all-to-all-done.1 = f32[128,1,128]{2,1,0:T(1,128)S(1)} async-done(((f32[128,1,128]{2,1,0:T(1,128)}), f32[128,1,128]{2,1,0:T(1,128)S(1)}, u32[]{:S(2)}, u32[]{:S(2)}) %all-to-all-start.1) | async-done | bytes 65568 | tf_op jit(solution)/shard_map/all_to_all | solution.py:481
  40.7 0.0 copy-done.2
  40.7 0.0 copy-done.3
  40.7 5.4 %shard_map.71 = (f32[5,1024,128]{2,1,0:T(8,128)}, f32[128,128]{1,0:T(8,128)}) custom-call(s32[8,128]{1,0:T(8,128)S(1)} %bitcast.23, s32[8,128]{1,0:T(8,128)S(1)} %get-tuple-element.20.rank_ref, s32[8,128]{1,0:T(8,128)S(1)} %bitcast.24, f32[128,128]{1,0:T(8,128)S(1)} %bitcast.21, f32[5,1024,128]{2,1,0:T(8,128)} %old_ref.1), custom_call_target="tpu_custom_call" | custom-call | flops 10000000000 | bytes 5242880 | tf_op jit(solution)/shard_map/pallas_call | solution.py:493
  46.1 4.6 %all-to-all-start.2 = ((f32[128,1,128]{2,1,0:T(1,128)}), f32[128,1,128]{2,1,0:T(1,128)S(1)}, u32[]{:S(2)}, u32[]{:S(2)}) async-start(f32[128,1,128]{2,1,0:T(1,128)} %bitcast.10), calls=%async_computation.2 | async-start | bytes 131072 | tf_op jit(solution)/shard_map/all_to_all | solution.py:481
  50.7 0.0 collective-permute-done.3.low
  50.7 0.0 collective-permute-done.4.high
  50.7 6.8 %shard_map.73 = f32[6,4,32,256]{3,2,1,0:T(8,128)S(1)} custom-call(f32[6,4,32,256]{3,2,1,0:T(8,128)S(1)} %copy-done.1, f32[6,4,8,256]{3,2,1,0:T(8,128)S(1)} %collective-permute-done.edge_ref, f32[6,32,256]{2,1,0:T(8,128)S(1)} %collective-permute-done.1.below, f32[6,32,256]{2,1,0:T(8,128)S(1)} %collective-permute-done.2.above, ...), custom_call_target="tpu_custom_call" | custom-call | flops 1 | bytes 1 | tf_op jit(solution)/shard_map/pallas_call | solution.py:566
  57.6 2.7 %all-to-all-done.2 = f32[128,1,128]{2,1,0:T(1,128)S(1)} async-done(((f32[128,1,128]{2,1,0:T(1,128)}), f32[128,1,128]{2,1,0:T(1,128)S(1)}, u32[]{:S(2)}, u32[]{:S(2)}) %all-to-all-start.2) | async-done | bytes 65568 | tf_op jit(solution)/shard_map/all_to_all | solution.py:481
  60.3 2.5 %shard_map.74 = f32[6,128,256]{2,1,0:T(8,128)} custom-call(s32[128,128]{1,0:T(8,128)S(1)} %bitcast.19, f32[128,128]{1,0:T(8,128)S(1)} %bitcast.20, f32[6,128,256]{2,1,0:T(8,128)S(1)} %bitcast.17), custom_call_target="tpu_custom_call" | custom-call | flops 1 | bytes 1 | tf_op jit(solution)/shard_map/pallas_call | solution.py:579
Async XLA Ops:
  2.7 22.2 %all-to-all-start = ((s32[128,1,128]{2,1,0:T(1,128)}), s32[128,1,128]{2,1,0:T(1,128)S(1)}, u32[]{:S(2)}, u32[]{:S(2)}) async-start(s32[128,1,128]{2,1,0:T(1,128)} %bitcast.3), calls=%async_computation | async-start | bytes 131072 | tf_op jit(solution)/shard_map/all_to_all | solution.py:481
  15.1 16.1 %collective-permute-start = (f32[6,4,8,256]{3,2,1,0:T(8,128)S(1)}, f32[6,4,8,256]{3,2,1,0:T(8,128)S(1)}, u32[]{:S(2)}, u32[]{:S(2)}) collective-permute-start(f32[6,4,8,256]{3,2,1,0:T(8,128)S(1)} %constant_dynamic-slice_fusion), channel_id=1, source_target_pairs={{0,1},{1,0},{2,3},{3,2},{4,5},{5,4},{6,7},{7,6},{8,9},{9,8},{10,11... | collective-permute-start | bytes 589832 | tf_op jit(solution)/shard_map/ppermute | solution.py:540
  16.3 1.1 %copy-start = (f32[6,4,32,256]{3,2,1,0:T(8,128)S(1)}, f32[6,4,32,256]{3,2,1,0:T(8,128)}, u32[]{:S(2)}) copy-start(f32[6,4,32,256]{3,2,1,0:T(8,128)} %gas_ref.4) | copy-start | bytes 2359300
  17.4 13.9 %copy-start.1 = (f32[6,4,32,256]{3,2,1,0:T(8,128)S(1)}, f32[6,4,32,256]{3,2,1,0:T(8,128)}, u32[]{:S(2)}) copy-start(f32[6,4,32,256]{3,2,1,0:T(8,128)} %gas_ref.4) | copy-start | bytes 2359300
  17.4 23.3 %copy-start.2 = (s32[1024,1]{0,1:T(1,128)S(1)}, s32[1024,1]{0,1:T(1,128)}, u32[]{:S(2)}) copy-start(s32[1024,1]{0,1:T(1,128)} %param.7) | copy-start | bytes 12292
  17.4 23.3 %copy-start.3 = (s32[1024]{0:T(1024)S(1)}, s32[1024]{0:T(1024)}, u32[]{:S(2)}) copy-start(s32[1024]{0:T(1024)} %param.9) | copy-start | bytes 12292
  17.7 13.6 %collective-permute-start.1 = (f32[6,32,256]{2,1,0:T(8,128)S(1)}, f32[6,32,256]{2,1,0:T(8,128)S(1)}, u32[]{:S(2)}, u32[]{:S(2)}) collective-permute-start(f32[6,32,256]{2,1,0:T(8,128)S(1)} %get-tuple-element.24), channel_id=1, source_target_pairs={{0,2},{2,4},{4,6},{6,8},{8,10},{10,12},{12,14},{14,16},{16,18},{18... | collective-permute-start | bytes 589832 | tf_op jit(solution)/shard_map/ppermute | solution.py:547
  18.6 12.7 %collective-permute-start.2 = (f32[6,32,256]{2,1,0:T(8,128)S(1)}, f32[6,32,256]{2,1,0:T(8,128)S(1)}, u32[]{:S(2)}, u32[]{:S(2)}) collective-permute-start(f32[6,32,256]{2,1,0:T(8,128)S(1)} %get-tuple-element.25), channel_id=1, source_target_pairs={{2,0},{4,2},{6,4},{8,6},{10,8},{12,10},{14,12},{16,14},{18,16},{20... | collective-permute-start | bytes 589832 | tf_op jit(solution)/shard_map/ppermute | solution.py:548
  27.4 13.3 %all-to-all-start.1 = ((f32[128,1,128]{2,1,0:T(1,128)}), f32[128,1,128]{2,1,0:T(1,128)S(1)}, u32[]{:S(2)}, u32[]{:S(2)}) async-start(f32[128,1,128]{2,1,0:T(1,128)} %bitcast.7), calls=%async_computation.1 | async-start | bytes 131072 | tf_op jit(solution)/shard_map/all_to_all | solution.py:481
  32.1 18.6 %collective-permute-start.3 = (f32[6,72,256]{2,1,0:T(8,128)}, f32[6,72,256]{2,1,0:T(8,128)S(1)}, u32[]{:S(2)}, u32[]{:S(2)}) collective-permute-start(f32[6,72,256]{2,1,0:T(8,128)} %get-tuple-element.29), channel_id=1, source_target_pairs={{0,2},{2,4},{4,6},{6,8},{8,10},{10,12},{12,14},{14,16},{16,18},{18... | collective-permute-start | bytes 1327112 | tf_op jit(solution)/shard_map/ppermute | solution.py:557
  33.8 17.0 %collective-permute-start.4 = (f32[6,72,256]{2,1,0:T(8,128)S(1)}, f32[6,72,256]{2,1,0:T(8,128)S(1)}, u32[]{:S(2)}, u32[]{:S(2)}) collective-permute-start(f32[6,72,256]{2,1,0:T(8,128)S(1)} %get-tuple-element.30), channel_id=1, source_target_pairs={{2,0},{4,2},{6,4},{8,6},{10,8},{12,10},{14,12},{16,14},{18,16},{20... | collective-permute-start | bytes 1327112 | tf_op jit(solution)/shard_map/ppermute | solution.py:558
  46.1 14.1 %all-to-all-start.2 = ((f32[128,1,128]{2,1,0:T(1,128)}), f32[128,1,128]{2,1,0:T(1,128)S(1)}, u32[]{:S(2)}, u32[]{:S(2)}) async-start(f32[128,1,128]{2,1,0:T(1,128)} %bitcast.10), calls=%async_computation.2 | async-start | bytes 131072 | tf_op jit(solution)/shard_map/all_to_all | solution.py:481

commit v4 on v3

--- a/solution.py
+++ b/solution.py
@@ -19,6 +19,8 @@
 HALO = 3
 FAR = HALO - 1
 PART = 256
+GATHERED = 2
+SCATTERED = 2
 PARCEL_FLOPS = 10**10
 EXT_X = CX + 2 * HALO
 EXT_Y = CY + 8
@@ -99,12 +101,15 @@
         pl.when(pair == core)(lambda: action(core, *refs))
 
 
-def table_kernel(gas_ref, table_ref, first_ref, second_ref):
-    def outermost(pair, up_ref, down_ref):
-        up_ref[...] = gas_ref[:, CX - 1]
-        down_ref[...] = gas_ref[:, 0]
-
-    by_core(outermost, first_ref, second_ref)
+def table_kernel(gas_ref, table_ref, up_ref, down_ref, edge_ref):
+    up_ref[...] = gas_ref[:, CX - 1]
+    down_ref[...] = gas_ref[:, 0]
+
+    def beside(pair):
+        start = (1 - pair) * (CY - 8)
+        edge_ref[...] = gas_ref[:, :, start : start + 8]
+
+    by_core(beside)
     inverse = 1.0 / gas_ref[0].reshape(ROWS, NZ)
     for c in range(NVAR):
         value = gas_ref[1 + c].reshape(ROWS, NZ) * inverse
@@ -142,18 +147,18 @@
     row, lane = cell_parts(asked_ref)
     table = table_ref[...]
     found[...] = jnp.zeros((LANES, LANES), F32)
-    for pair in range(CAP // 2):
-        k = 2 * pair
-        rows = jnp.concatenate([row[k : k + 1], row[k + 1 : k + 2]], axis=1)
-        lanes = jnp.concatenate([lane[k : k + 1], lane[k + 1 : k + 2]], axis=1)
-        hot = ones_where(iota((2 * ROWS, 2 * LANES), 0) == rows)
+    for k in range(0, CAP, GATHERED):
+        rows = jnp.concatenate([row[k + j : k + j + 1] for j in range(GATHERED)], axis=1)
+        lanes = jnp.concatenate([lane[k + j : k + j + 1] for j in range(GATHERED)], axis=1)
+        hot = ones_where(iota((2 * ROWS, GATHERED * LANES), 0) == rows)
         values = dot(table, jnp.concatenate([hot] * PIECES, axis=0))
-        here = iota((LANES, 2 * LANES), 0) == lanes
+        here = iota((LANES, GATHERED * LANES), 0) == lanes
         for c in range(NVAR):
             part = values[c * LANES : (c + 1) * LANES]
             picked = jnp.sum(jnp.where(here, part, 0.0), axis=0, keepdims=True)
-            found[c * CAP + k : c * CAP + k + 1, :] = picked[:, :LANES]
-            found[c * CAP + k + 1 : c * CAP + k + 2, :] = picked[:, LANES:]
+            for j in range(GATHERED):
+                at = c * CAP + k + j
+                found[at : at + 1, :] = picked[:, j * LANES : (j + 1) * LANES]
     reply_ref[...] = found[...].T
 
 
@@ -182,7 +187,7 @@
 
 def parcel_kernel(
     owner_ref, rank_ref, live_ref, ans_ref, old_ref, new_ref, send_ref,
-    held, made, hot, turned, slots, alive, spread, placed, outgoing, got, sent, posted,
+    held, made, hot, turned, slots, alive, spread, placed, outgoing, gas_wide, got, sent, posted,
 ):
     parts = BLK_DEV // PART
     fetches = []
@@ -197,28 +202,30 @@
     columns = stack.T.astype(BF16)
     across = iota((LANES, LANES), 1)
     down = iota((LANES, LANES), 0)
+    acrossf = across.astype(F32)
+    slotf = (across % CAP).astype(F32)
     for i in range(CHUNKS):
         shape = (LANES, 3 * LANES)
         chosen = ones_where(iota(shape, 0) == i + CHUNKS * (iota(shape, 1) // LANES))
-        wide = dot(columns, chosen).astype(jnp.int32)
+        wide = dot(columns, chosen)
         owner, rank, live = (wide[:, s * LANES : (s + 1) * LANES] for s in range(3))
         here = slice(i * LANES, (i + 1) * LANES)
-        hot[here, :] = ones_where(owner == across)
-        slots[here, :] = ones_where(across % CAP == rank)
-        alive[here, :] = jnp.where(across < live, 1.0, 0.0)
+        hot[here, :] = ones_where(owner == acrossf)
+        slots[here, :] = ones_where(slotf == rank)
+        alive[here, :] = jnp.where(acrossf < live, 1.0, 0.0)
         turned[:, here] = ones_where(down == owner_ref[i : i + 1, :])
     shape = (PIECES * LANES, NVAR * LANES)
     spread[...] = ones_where((iota(shape, 0) % LANES) // CAP == iota(shape, 1) // LANES)
 
     answers = jnp.concatenate(split(ans_ref[...]), axis=1)
+    received = dot(hot[...], answers).astype(BF16)
+    gas_wide[...] = dot(received * jnp.concatenate([slots[...]] * PIECES, axis=1), spread[...])
     kind = iota((PART, LANES), 1) // CAP
     stores = []
     for part in range(parts):
         here = slice(part * PART, (part + 1) * PART)
         slot = slots[here, :]
-        received = dot(hot[here, :], answers).astype(BF16)
-        wide = dot(received * jnp.concatenate([slot] * PIECES, axis=1), spread[...])
-        gas_vars = [wide[:, c * LANES : (c + 1) * LANES] for c in range(NVAR)]
+        gas_vars = [gas_wide[here, c * LANES : (c + 1) * LANES] for c in range(NVAR)]
         fetches[part].wait()
         old = [held[c, here, :] for c in range(5)]
         living = alive[here, :] > 0.0
@@ -227,6 +234,11 @@
             made[c, here, :] = new[c]
         stores.append(pltpu.make_async_copy(made.at[:, here, :], new_ref.at[:, here, :], sent.at[part]))
         stores[part].start()
+    for part in range(parts):
+        here = slice(part * PART, (part + 1) * PART)
+        slot = slots[here, :]
+        old = [held[c, here, :] for c in range(5)]
+        new = [made[c, here, :] for c in range(5)]
         change = [old[0] - new[0]] + [old[0] * old[c] - new[0] * new[c] for c in range(1, 5)]
         total = jnp.zeros((PART, LANES), F32)
         for c in range(NVAR):
@@ -245,9 +257,9 @@
 def scatter_kernel(asked_ref, come_ref, section_ref, out_ref, total, made, sent):
     row, lane = cell_parts(asked_ref)
     pieces = [p.astype(F32) for p in split(come_ref[...].T)]
-    for pair in range(CAP // 2):
+    for start in range(0, CAP, SCATTERED):
         hots, parts = [], []
-        for k in (2 * pair, 2 * pair + 1):
+        for k in range(start, start + SCATTERED):
             hot = ones_where(iota((2 * ROWS, LANES), 0) == row[k : k + 1])
             here = iota((LANES, LANES), 0) == lane[k : k + 1]
             for piece in pieces:
@@ -262,7 +274,7 @@
                     ).astype(BF16)
                 )
         added = dot_nt(jnp.concatenate(parts, axis=1), jnp.concatenate(hots, axis=1))
-        if pair == 0:
+        if start == 0:
             total[...] = added
         else:
             total[...] += added
@@ -507,6 +519,7 @@
             pltpu.VMEM((PIECES * LANES, NVAR * LANES), BF16),
             pltpu.VMEM((BLK_DEV, PIECES * LANES), BF16),
             pltpu.VMEM((DEVICES, LANES), F32),
+            pltpu.VMEM((BLK_DEV, NVAR * LANES), F32),
             pltpu.SemaphoreType.DMA((BLK_DEV // PART,)),
             pltpu.SemaphoreType.DMA((BLK_DEV // PART,)),
             pltpu.SemaphoreType.DMA,
@@ -536,14 +549,20 @@
     asked = deliver(requests)
 
     mine, _ = lax.optimization_barrier((gas_state, requests))
-    edge = lax.dynamic_slice_in_dim(mine, (1 - pair) * (CY - 8), 8, axis=2)
-    edge = lax.ppermute(edge, "grp", [(0, 1), (1, 0)])
     circuit = [(i, (i + 1) % count) for i in range(count)]
     back = [(target, source) for source, target in circuit]
     row = jax.ShapeDtypeStruct((6, CY, NZ), F32)
-    table, first, second = call(
-        table_kernel, 12, [jax.ShapeDtypeStruct((NVAR * LANES, PIECES * 2 * ROWS), BF16), row, row]
+    table, first, second, edge = call(
+        table_kernel,
+        12,
+        [
+            jax.ShapeDtypeStruct((NVAR * LANES, PIECES * 2 * ROWS), BF16),
+            row,
+            row,
+            jax.ShapeDtypeStruct((6, CX, 8, NZ), F32),
+        ],
     )(mine)
+    edge = lax.ppermute(edge, "grp", [(0, 1), (1, 0)])
     below = lax.ppermute(first, "gas", circuit)
     above = lax.ppermute(second, "gas", back)
     replies = call(gather_kernel, 16, square, [pltpu.VMEM((LANES, LANES), F32)], cost=LARGE)(asked, table)

time: 63.1 us -> 62.2 us (0.986)
  local copies, waits for them, and re-layouts: 2.09 us -> 1.14 us
    dynamic_slice x1 -> x0, local copies, waits for them, and re-layouts: 0.95 us -> none  [body(): edge = lax.dynamic_slice_in_dim(mine, (1 - pair) * (CY - 8), 8, axis=2)]
  transfers between devices with their start and end apart: 8 -> 8, of which waited for: 2 -> 2; matrix products, arithmetic and copies ran while one was open for 2% -> 0% of each run, Pallas kernels for 25% -> 25%
where the time goes in v4:
time: 62.2 us; the launch traced here: 61.9 us
  starting transfers between devices  36.4 us (59%)
  Pallas kernels  20.2 us (32%)
  waiting for transfers between devices  3.41 us (5%)
  local copies, waits for them, and re-layouts  1.14 us (2%)
  between operations  0.74 us (1%)
    all_to_all x3, starting transfers between devices, deliver(): return lax.all_to_all(buffer, AXES, split_axis=0, concat_axis=0, tiled=True)  20.4 us
    pallas_call x1, Pallas kernels, body(): call(gas_kernel, 28, jax.ShapeDtypeStruct((6, CX, CY, NZ), F32), [extende...  6.83 us
    ppermute x1, starting transfers between devices, body(): above = lax.ppermute(second, 'gas', back)  6.22 us
    ppermute x1, starting transfers between devices, body(): high = lax.ppermute(second, 'gas', back)  6.22 us
    pallas_call x1, Pallas kernels, integrate_parcels(): call(parcel_kernel, 24, [jax.ShapeDtypeStruct((5, BLK_DEV, LANES), F32),...  5.18 us
    all_to_all x3, waiting for transfers between devices, deliver(): return lax.all_to_all(buffer, AXES, split_axis=0, concat_axis=0, tiled=True)  3.39 us
    pallas_call x1, Pallas kernels, body(): call(gather_kernel, 16, square, [pltpu.VMEM((LANES, LANES), F32)], cost=L...  2.53 us
    pallas_call x1, Pallas kernels, body(): call(scatter_kernel, 20, jax.ShapeDtypeStruct((6, ROWS, NZ), F32), [pltpu...  2.49 us
  transfers between devices with their start and end apart: 8, of which 2 were waited for; matrix products, arithmetic and copies ran while one was open for 0% of the time, Pallas kernels for 25%

profile of v4, /device:TPU:1, one launch (start us, length us, event | category | flops | bytes accessed | tf_op | source)
XLA Modules:
  0.0 61.9 jit_solution(17877892861958503334)
XLA Ops:
  0.6 2.0 %shard_map.68 = (s32[128,128]{1,0:T(8,128)}, s32[8,128]{1,0:T(8,128)S(1)}) custom-call(s32[8,128]{1,0:T(8,128)} %bitcast.22, s32[8,128]{1,0:T(8,128)} %bitcast.26), custom_call_target="tpu_custom_call" | custom-call | flops 1 | bytes 1 | tf_op jit(solution)/shard_map/pallas_call | solution.py:541
  2.7 11.5 %all-to-all-start = ((s32[128,1,128]{2,1,0:T(1,128)}), s32[128,1,128]{2,1,0:T(1,128)S(1)}, u32[]{:S(2)}, u32[]{:S(2)}) async-start(s32[128,1,128]{2,1,0:T(1,128)} %bitcast.3), calls=%async_computation | async-start | bytes 131072 | tf_op jit(solution)/shard_map/all_to_all | solution.py:493
  14.2 0.0 copy-start
  14.2 1.1 %copy-done = f32[6,4,32,256]{3,2,1,0:T(8,128)S(1)} copy-done((f32[6,4,32,256]{3,2,1,0:T(8,128)S(1)}, f32[6,4,32,256]{3,2,1,0:T(8,128)}, u32[]{:S(2)}) %copy-start) | copy-done | bytes 786456
  15.3 0.0 copy-start.1
  15.3 0.0 copy-start.2
  15.3 0.0 copy-start.3
  15.3 0.3 shard_map.69
  15.6 1.1 %collective-permute-start = (f32[6,4,8,256]{3,2,1,0:T(8,128)S(1)}, f32[6,4,8,256]{3,2,1,0:T(8,128)S(1)}, u32[]{:S(2)}, u32[]{:S(2)}) collective-permute-start(f32[6,4,8,256]{3,2,1,0:T(8,128)S(1)} %get-tuple-element.25), channel_id=1, source_target_pairs={{0,1},{1,0},{2,3},{3,2},{4,5},{5,4},{6,7},{7,6},{8,9},{9,8},{10,11... | collective-permute-start | bytes 589832 | tf_op jit(solution)/shard_map/ppermute | solution.py:565
  16.8 0.8 %collective-permute-start.1 = (f32[6,32,256]{2,1,0:T(8,128)S(1)}, f32[6,32,256]{2,1,0:T(8,128)S(1)}, u32[]{:S(2)}, u32[]{:S(2)}) collective-permute-start(f32[6,32,256]{2,1,0:T(8,128)S(1)} %get-tuple-element.26), channel_id=1, source_target_pairs={{0,2},{2,4},{4,6},{6,8},{8,10},{10,12},{12,14},{14,16},{16,18},{18... | collective-permute-start | bytes 589832 | tf_op jit(solution)/shard_map/ppermute | solution.py:566
  17.6 6.2 %collective-permute-start.2 = (f32[6,32,256]{2,1,0:T(8,128)S(1)}, f32[6,32,256]{2,1,0:T(8,128)S(1)}, u32[]{:S(2)}, u32[]{:S(2)}) collective-permute-start(f32[6,32,256]{2,1,0:T(8,128)S(1)} %get-tuple-element.27), channel_id=1, source_target_pairs={{2,0},{4,2},{6,4},{8,6},{10,8},{12,10},{14,12},{16,14},{18,16},{20... | collective-permute-start | bytes 589832 | tf_op jit(solution)/shard_map/ppermute | solution.py:567
  23.8 0.0 all-to-all-done
  23.8 2.5 %shard_map.70 = f32[128,128]{1,0:T(8,128)} custom-call(s32[128,128]{1,0:T(8,128)S(1)} %bitcast.18, bf16[640,512]{1,0:T(8,128)(2,1)S(1)} %get-tuple-element.23.table_ref), custom_call_target="tpu_custom_call" | custom-call | flops 1000000000 | bytes 1 | tf_op jit(solution)/shard_map/pallas_call | solution.py:568
  26.3 4.3 %all-to-all-start.1 = ((f32[128,1,128]{2,1,0:T(1,128)}), f32[128,1,128]{2,1,0:T(1,128)S(1)}, u32[]{:S(2)}, u32[]{:S(2)}) async-start(f32[128,1,128]{2,1,0:T(1,128)} %bitcast.7), calls=%async_computation.1 | async-start | bytes 131072 | tf_op jit(solution)/shard_map/all_to_all | solution.py:493
  30.7 0.0 collective-permute-done.edge_ref
  30.7 0.0 collective-permute-done.1.below
  30.7 0.0 collective-permute-done.2.above
  30.7 0.0 copy-done.1
  30.7 0.8 %shard_map.72 = (f32[6,72,256]{2,1,0:T(8,128)}, f32[6,72,256]{2,1,0:T(8,128)S(1)}) custom-call(f32[6,4,32,256]{3,2,1,0:T(8,128)S(1)} %copy-done.1, f32[6,4,8,256]{3,2,1,0:T(8,128)S(1)} %collective-permute-done.edge_ref), custom_call_target="tpu_custom_call" | custom-call | flops 1 | bytes 1 | tf_op jit(solution)/shard_map/pallas_call | solution.py:575
  31.5 1.6 %collective-permute-start.3 = (f32[6,72,256]{2,1,0:T(8,128)}, f32[6,72,256]{2,1,0:T(8,128)S(1)}, u32[]{:S(2)}, u32[]{:S(2)}) collective-permute-start(f32[6,72,256]{2,1,0:T(8,128)} %get-tuple-element.31), channel_id=1, source_target_pairs={{0,2},{2,4},{4,6},{6,8},{8,10},{10,12},{12,14},{14,16},{16,18},{18... | collective-permute-start | bytes 1327112 | tf_op jit(solution)/shard_map/ppermute | solution.py:576
  33.1 6.2 %collective-permute-start.4 = (f32[6,72,256]{2,1,0:T(8,128)S(1)}, f32[6,72,256]{2,1,0:T(8,128)S(1)}, u32[]{:S(2)}, u32[]{:S(2)}) collective-permute-start(f32[6,72,256]{2,1,0:T(8,128)S(1)} %get-tuple-element.32), channel_id=1, source_target_pairs={{2,0},{4,2},{6,4},{8,6},{10,8},{12,10},{14,12},{16,14},{18,16},{20... | collective-permute-start | bytes 1327112 | tf_op jit(solution)/shard_map/ppermute | solution.py:577
  39.4 0.7 %all-to-all-done.1 = f32[128,1,128]{2,1,0:T(1,128)S(1)} async-done(((f32[128,1,128]{2,1,0:T(1,128)}), f32[128,1,128]{2,1,0:T(1,128)S(1)}, u32[]{:S(2)}, u32[]{:S(2)}) %all-to-all-start.1) | async-done | bytes 65568 | tf_op jit(solution)/shard_map/all_to_all | solution.py:493
  40.1 0.0 copy-done.2
  40.1 0.0 copy-done.3
  40.1 5.2 %shard_map.71 = (f32[5,1024,128]{2,1,0:T(8,128)}, f32[128,128]{1,0:T(8,128)}) custom-call(s32[8,128]{1,0:T(8,128)S(1)} %bitcast.23, s32[8,128]{1,0:T(8,128)S(1)} %get-tuple-element.21.rank_ref, s32[8,128]{1,0:T(8,128)S(1)} %bitcast.24, f32[128,128]{1,0:T(8,128)S(1)} %bitcast.21, f32[5,1024,128]{2,1,0:T(8,128)} %old_ref.1), custom_call_target="tpu_custom_call" | custom-call | flops 10000000000 | bytes 5242880 | tf_op jit(solution)/shard_map/pallas_call | solution.py:505
  45.3 4.6 %all-to-all-start.2 = ((f32[128,1,128]{2,1,0:T(1,128)}), f32[128,1,128]{2,1,0:T(1,128)S(1)}, u32[]{:S(2)}, u32[]{:S(2)}) async-start(f32[128,1,128]{2,1,0:T(1,128)} %bitcast.10), calls=%async_computation.2 | async-start | bytes 131072 | tf_op jit(solution)/shard_map/all_to_all | solution.py:493
  49.9 0.0 collective-permute-done.3.low
  49.9 0.0 collective-permute-done.4.high
  49.9 6.8 %shard_map.73 = f32[6,4,32,256]{3,2,1,0:T(8,128)S(1)} custom-call(f32[6,4,32,256]{3,2,1,0:T(8,128)S(1)} %copy-done.1, f32[6,4,8,256]{3,2,1,0:T(8,128)S(1)} %collective-permute-done.edge_ref, f32[6,32,256]{2,1,0:T(8,128)S(1)} %collective-permute-done.1.below, f32[6,32,256]{2,1,0:T(8,128)S(1)} %collective-permute-done.2.above, ...), custom_call_target="tpu_custom_call" | custom-call | flops 1 | bytes 1 | tf_op jit(solution)/shard_map/pallas_call | solution.py:585
  56.7 2.7 %all-to-all-done.2 = f32[128,1,128]{2,1,0:T(1,128)S(1)} async-done(((f32[128,1,128]{2,1,0:T(1,128)}), f32[128,1,128]{2,1,0:T(1,128)S(1)}, u32[]{:S(2)}, u32[]{:S(2)}) %all-to-all-start.2) | async-done | bytes 65568 | tf_op jit(solution)/shard_map/all_to_all | solution.py:493
  59.4 2.5 %shard_map.74 = f32[6,128,256]{2,1,0:T(8,128)} custom-call(s32[128,128]{1,0:T(8,128)S(1)} %bitcast.19, f32[128,128]{1,0:T(8,128)S(1)} %bitcast.20, f32[6,128,256]{2,1,0:T(8,128)S(1)} %bitcast.17), custom_call_target="tpu_custom_call" | custom-call | flops 1 | bytes 1 | tf_op jit(solution)/shard_map/pallas_call | solution.py:598
Async XLA Ops:
  2.7 21.1 %all-to-all-start = ((s32[128,1,128]{2,1,0:T(1,128)}), s32[128,1,128]{2,1,0:T(1,128)S(1)}, u32[]{:S(2)}, u32[]{:S(2)}) async-start(s32[128,1,128]{2,1,0:T(1,128)} %bitcast.3), calls=%async_computation | async-start | bytes 131072 | tf_op jit(solution)/shard_map/all_to_all | solution.py:493
  14.2 1.1 %copy-start = (f32[6,4,32,256]{3,2,1,0:T(8,128)S(1)}, f32[6,4,32,256]{3,2,1,0:T(8,128)}, u32[]{:S(2)}) copy-start(f32[6,4,32,256]{3,2,1,0:T(8,128)} %gas_ref.4) | copy-start | bytes 2359300
  15.3 15.4 %copy-start.1 = (f32[6,4,32,256]{3,2,1,0:T(8,128)S(1)}, f32[6,4,32,256]{3,2,1,0:T(8,128)}, u32[]{:S(2)}) copy-start(f32[6,4,32,256]{3,2,1,0:T(8,128)} %gas_ref.4) | copy-start | bytes 2359300
  15.3 24.8 %copy-start.2 = (s32[1024,1]{0,1:T(1,128)S(1)}, s32[1024,1]{0,1:T(1,128)}, u32[]{:S(2)}) copy-start(s32[1024,1]{0,1:T(1,128)} %param.7) | copy-start | bytes 12292
  15.3 24.8 %copy-start.3 = (s32[1024]{0:T(1024)S(1)}, s32[1024]{0:T(1024)}, u32[]{:S(2)}) copy-start(s32[1024]{0:T(1024)} %param.9) | copy-start | bytes 12292
  15.6 15.1 %collective-permute-start = (f32[6,4,8,256]{3,2,1,0:T(8,128)S(1)}, f32[6,4,8,256]{3,2,1,0:T(8,128)S(1)}, u32[]{:S(2)}, u32[]{:S(2)}) collective-permute-start(f32[6,4,8,256]{3,2,1,0:T(8,128)S(1)} %get-tuple-element.25), channel_id=1, source_target_pairs={{0,1},{1,0},{2,3},{3,2},{4,5},{5,4},{6,7},{7,6},{8,9},{9,8},{10,11... | collective-permute-start | bytes 589832 | tf_op jit(solution)/shard_map/ppermute | solution.py:565
  16.8 13.9 %collective-permute-start.1 = (f32[6,32,256]{2,1,0:T(8,128)S(1)}, f32[6,32,256]{2,1,0:T(8,128)S(1)}, u32[]{:S(2)}, u32[]{:S(2)}) collective-permute-start(f32[6,32,256]{2,1,0:T(8,128)S(1)} %get-tuple-element.26), channel_id=1, source_target_pairs={{0,2},{2,4},{4,6},{6,8},{8,10},{10,12},{12,14},{14,16},{16,18},{18... | collective-permute-start | bytes 589832 | tf_op jit(solution)/shard_map/ppermute | solution.py:566
  17.6 13.1 %collective-permute-start.2 = (f32[6,32,256]{2,1,0:T(8,128)S(1)}, f32[6,32,256]{2,1,0:T(8,128)S(1)}, u32[]{:S(2)}, u32[]{:S(2)}) collective-permute-start(f32[6,32,256]{2,1,0:T(8,128)S(1)} %get-tuple-element.27), channel_id=1, source_target_pairs={{2,0},{4,2},{6,4},{8,6},{10,8},{12,10},{14,12},{16,14},{18,16},{20... | collective-permute-start | bytes 589832 | tf_op jit(solution)/shard_map/ppermute | solution.py:567
  26.3 13.8 %all-to-all-start.1 = ((f32[128,1,128]{2,1,0:T(1,128)}), f32[128,1,128]{2,1,0:T(1,128)S(1)}, u32[]{:S(2)}, u32[]{:S(2)}) async-start(f32[128,1,128]{2,1,0:T(1,128)} %bitcast.7), calls=%async_computation.1 | async-start | bytes 131072 | tf_op jit(solution)/shard_map/all_to_all | solution.py:493
  31.5 18.3 %collective-permute-start.3 = (f32[6,72,256]{2,1,0:T(8,128)}, f32[6,72,256]{2,1,0:T(8,128)S(1)}, u32[]{:S(2)}, u32[]{:S(2)}) collective-permute-start(f32[6,72,256]{2,1,0:T(8,128)} %get-tuple-element.31), channel_id=1, source_target_pairs={{0,2},{2,4},{4,6},{6,8},{8,10},{10,12},{12,14},{14,16},{16,18},{18... | collective-permute-start | bytes 1327112 | tf_op jit(solution)/shard_map/ppermute | solution.py:576
  33.1 16.8 %collective-permute-start.4 = (f32[6,72,256]{2,1,0:T(8,128)S(1)}, f32[6,72,256]{2,1,0:T(8,128)S(1)}, u32[]{:S(2)}, u32[]{:S(2)}) collective-permute-start(f32[6,72,256]{2,1,0:T(8,128)S(1)} %get-tuple-element.32), channel_id=1, source_target_pairs={{2,0},{4,2},{6,4},{8,6},{10,8},{12,10},{14,12},{16,14},{18,16},{20... | collective-permute-start | bytes 1327112 | tf_op jit(solution)/shard_map/ppermute | solution.py:577
  45.3 14.1 %all-to-all-start.2 = ((f32[128,1,128]{2,1,0:T(1,128)}), f32[128,1,128]{2,1,0:T(1,128)S(1)}, u32[]{:S(2)}, u32[]{:S(2)}) async-start(f32[128,1,128]{2,1,0:T(1,128)} %bitcast.10), calls=%async_computation.2 | async-start | bytes 131072 | tf_op jit(solution)/shard_map/all_to_all | solution.py:493

commit v5 on v4

--- a/solution.py
+++ b/solution.py
@@ -185,9 +185,29 @@
     return [mass * jnp.exp2(1.5 * (first_power - power))] + moved + [thermal]
 
 
+def prepare_kernel(owner_ref, rank_ref, live_ref, hot_ref, turned_ref, code_ref):
+    pad = jnp.zeros((LANES - 3 * CHUNKS, LANES), F32)
+    rows = [owner_ref[...], rank_ref[...], live_ref[...]]
+    stack = jnp.concatenate([r.astype(F32) for r in rows] + [pad], axis=0)
+    columns = stack.T.astype(BF16)
+    across, down = iota((LANES, LANES), 1), iota((LANES, LANES), 0)
+    lane = across.astype(F32)
+    lane_slot = (across % CAP).astype(F32)
+    for i in range(CHUNKS):
+        shape = (LANES, 3 * LANES)
+        chosen = ones_where(iota(shape, 0) == i + CHUNKS * (iota(shape, 1) // LANES))
+        wide = dot(columns, chosen)
+        owner, rank, live = (wide[:, s * LANES : (s + 1) * LANES] for s in range(3))
+        here = slice(i * LANES, (i + 1) * LANES)
+        hot_ref[here, :] = ones_where(owner == lane)
+        code = jnp.where(lane_slot == rank, 1.0, 0.0) + jnp.where(lane < live, 2.0, 0.0)
+        code_ref[here, :] = code.astype(BF16)
+        turned_ref[:, here] = ones_where(down == owner_ref[i : i + 1, :])
+
+
 def parcel_kernel(
-    owner_ref, rank_ref, live_ref, ans_ref, old_ref, new_ref, send_ref,
-    held, made, hot, turned, slots, alive, spread, placed, outgoing, gas_wide, got, sent, posted,
+    ans_ref, hot_ref, turned_ref, code_ref, old_ref, new_ref, send_ref,
+    held, made, spread, placed, outgoing, gas_wide, got, sent, posted,
 ):
     parts = BLK_DEV // PART
     fetches = []
@@ -196,39 +216,23 @@
         fetches.append(pltpu.make_async_copy(old_ref.at[:, here, :], held.at[:, here, :], got.at[part]))
         fetches[part].start()
 
-    pad = jnp.zeros((LANES - 3 * CHUNKS, LANES), F32)
-    rows = [owner_ref[...], rank_ref[...], live_ref[...]]
-    stack = jnp.concatenate([r.astype(F32) for r in rows] + [pad], axis=0)
-    columns = stack.T.astype(BF16)
-    across = iota((LANES, LANES), 1)
-    down = iota((LANES, LANES), 0)
-    acrossf = across.astype(F32)
-    slotf = (across % CAP).astype(F32)
-    for i in range(CHUNKS):
-        shape = (LANES, 3 * LANES)
-        chosen = ones_where(iota(shape, 0) == i + CHUNKS * (iota(shape, 1) // LANES))
-        wide = dot(columns, chosen)
-        owner, rank, live = (wide[:, s * LANES : (s + 1) * LANES] for s in range(3))
-        here = slice(i * LANES, (i + 1) * LANES)
-        hot[here, :] = ones_where(owner == acrossf)
-        slots[here, :] = ones_where(slotf == rank)
-        alive[here, :] = jnp.where(acrossf < live, 1.0, 0.0)
-        turned[:, here] = ones_where(down == owner_ref[i : i + 1, :])
     shape = (PIECES * LANES, NVAR * LANES)
     spread[...] = ones_where((iota(shape, 0) % LANES) // CAP == iota(shape, 1) // LANES)
 
     answers = jnp.concatenate(split(ans_ref[...]), axis=1)
-    received = dot(hot[...], answers).astype(BF16)
-    gas_wide[...] = dot(received * jnp.concatenate([slots[...]] * PIECES, axis=1), spread[...])
+    code = code_ref[...].astype(F32)
+    slots = jnp.where(code > 1.5, code - 2.0, code).astype(BF16)
+    received = dot(hot_ref[...], answers).astype(BF16)
+    gas_wide[...] = dot(received * jnp.concatenate([slots] * PIECES, axis=1), spread[...])
     kind = iota((PART, LANES), 1) // CAP
     stores = []
     for part in range(parts):
         here = slice(part * PART, (part + 1) * PART)
-        slot = slots[here, :]
+        slot = slots[here]
         gas_vars = [gas_wide[here, c * LANES : (c + 1) * LANES] for c in range(NVAR)]
         fetches[part].wait()
         old = [held[c, here, :] for c in range(5)]
-        living = alive[here, :] > 0.0
+        living = code_ref[here, :].astype(F32) > 1.5
         new = [jnp.where(living, n, o) for n, o in zip(integrate(old, gas_vars), old)]
         for c in range(5):
             made[c, here, :] = new[c]
@@ -236,7 +240,7 @@
         stores[part].start()
     for part in range(parts):
         here = slice(part * PART, (part + 1) * PART)
-        slot = slots[here, :]
+        slot = slots[here]
         old = [held[c, here, :] for c in range(5)]
         new = [made[c, here, :] for c in range(5)]
         change = [old[0] - new[0]] + [old[0] * old[c] - new[0] * new[c] for c in range(1, 5)]
@@ -245,7 +249,7 @@
             total = jnp.where(kind == c, jnp.sum(change[c], axis=1, keepdims=True), total)
         for p, piece in enumerate(split(total)):
             placed[here, p * LANES : (p + 1) * LANES] = piece * slot
-    send = dot(turned[...], placed[...])
+    send = dot(turned_ref[...], placed[...])
     outgoing[...] = sum(send[:, p * LANES : (p + 1) * LANES] for p in range(PIECES))
     post = pltpu.make_async_copy(outgoing, send_ref, posted)
     post.start()
@@ -501,7 +505,23 @@
     return pltpu.with_memory_space_constraint(array, pltpu.HBM)
 
 
-def integrate_parcels(owner, rank, live, answered, parcels):
+def in_vmem(array):
+    return pltpu.with_memory_space_constraint(array, pltpu.VMEM)
+
+
+def prepare(owner, rank, live):
+    return call(
+        prepare_kernel,
+        8,
+        [
+            pltpu.VMEM((BLK_DEV, DEVICES), BF16),
+            pltpu.VMEM((DEVICES, BLK_DEV), BF16),
+            pltpu.VMEM((BLK_DEV, LANES), BF16),
+        ],
+    )(owner, rank, live)
+
+
+def integrate_parcels(answered, prepared, parcels):
     return call(
         parcel_kernel,
         24,
@@ -512,10 +532,6 @@
         [
             pltpu.VMEM((5, BLK_DEV, LANES), F32),
             pltpu.VMEM((5, BLK_DEV, LANES), F32),
-            pltpu.VMEM((BLK_DEV, DEVICES), BF16),
-            pltpu.VMEM((DEVICES, BLK_DEV), BF16),
-            pltpu.VMEM((BLK_DEV, LANES), BF16),
-            pltpu.VMEM((BLK_DEV, LANES), F32),
             pltpu.VMEM((PIECES * LANES, NVAR * LANES), BF16),
             pltpu.VMEM((BLK_DEV, PIECES * LANES), BF16),
             pltpu.VMEM((DEVICES, LANES), F32),
@@ -527,7 +543,7 @@
         cost=pl.CostEstimate(flops=PARCEL_FLOPS, bytes_accessed=8 * 5 * BLK_DEV * LANES, transcendentals=0),
         in_specs=[HELD] * 4 + [ANYWHERE],
         out_specs=[ANYWHERE, ANYWHERE],
-    )(owner, rank, live, answered, in_hbm(parcels))
+    )(answered, *[in_vmem(p) for p in prepared], in_hbm(parcels))
 
 
 def body(gas_state, particle_blocks, owner, host_cell, live_count):
@@ -573,9 +589,11 @@
     )
     message = jax.ShapeDtypeStruct((6, FAR * CY + 8, NZ), F32)
     first, second = call(message_kernel, 12, [message, message])(gas_state, edge)
+    first, rank = lax.optimization_barrier((first, rank))
+    prepared = prepare(owner, rank, live)
     low = lax.ppermute(first, "gas", circuit)
     high = lax.ppermute(second, "gas", back)
-    parcels_next, sources = integrate_parcels(owner, rank, live, answered, particle_blocks)
+    parcels_next, sources = integrate_parcels(answered, prepared, particle_blocks)
     come = deliver(sources)
 
     below, above, low, high, _ = lax.optimization_barrier(
@@ -593,7 +611,7 @@
             pltpu.VMEM((4, EXT_X, EXT_Y, NZ), F32),
             pltpu.VMEM((6, EXT_Y, NZ), F32),
         ],
-    )(gas_state, edge, below, above, low, high)
+    )(in_hbm(gas_state), edge, below, above, low, high)
 
     gas_next = call(
         scatter_kernel,

time: 62.2 us -> 61.8 us (level)
  waiting for transfers between devices: 3.41 us -> 2.29 us
    pallas_call x1, Pallas kernels: 6.83 us -> 7.96 us  [body(): call(gas_kernel, 28, jax.ShapeDtypeStruct((6, CX, CY, NZ), F32), [extende...]
    all_to_all x3, waiting for transfers between devices: 3.39 us -> 2.28 us  [deliver(): return lax.all_to_all(buffer, AXES, split_axis=0, concat_axis=0, tiled=True)]
    pallas_call x1, Pallas kernels: 0.84 us -> 0.08 us  [body(): call(message_kernel, 12, [message, message])(gas_state, edge)]
  transfers between devices with their start and end apart: 8 -> 8, of which waited for: 2 -> 2; matrix products, arithmetic and copies ran while one was open for 0% -> 0% of each run, Pallas kernels for 25% -> 26%
where the time goes in v5:
time: 61.8 us; the launch traced here: 61.4 us
  starting transfers between devices  36.6 us (59%)
  Pallas kernels  20.7 us (33%)
  waiting for transfers between devices  2.29 us (4%)
  local copies, waits for them, and re-layouts  1.14 us (2%)
  between operations  0.76 us (1%)
    all_to_all x3, starting transfers between devices, deliver(): return lax.all_to_all(buffer, AXES, split_axis=0, concat_axis=0, tiled=True)  20.4 us
    pallas_call x1, Pallas kernels, body(): call(gas_kernel, 28, jax.ShapeDtypeStruct((6, CX, CY, NZ), F32), [extende...  7.96 us
    ppermute x1, starting transfers between devices, body(): high = lax.ppermute(second, 'gas', back)  6.3 us
    ppermute x1, starting transfers between devices, body(): above = lax.ppermute(second, 'gas', back)  6.22 us
    pallas_call x1, Pallas kernels, integrate_parcels(): call(parcel_kernel, 24, [jax.ShapeDtypeStruct((5, BLK_DEV, LANES), F32),...  4.84 us
    pallas_call x1, Pallas kernels, body(): call(gather_kernel, 16, square, [pltpu.VMEM((LANES, LANES), F32)], cost=L...  2.5 us
    pallas_call x1, Pallas kernels, body(): call(scatter_kernel, 20, jax.ShapeDtypeStruct((6, ROWS, NZ), F32), [pltpu...  2.49 us
    all_to_all x3, waiting for transfers between devices, deliver(): return lax.all_to_all(buffer, AXES, split_axis=0, concat_axis=0, tiled=True)  2.28 us
  transfers between devices with their start and end apart: 8, of which 2 were waited for; matrix products, arithmetic and copies ran while one was open for 0% of the time, Pallas kernels for 26%

profile of v5, /device:TPU:1, one launch (start us, length us, event | category | flops | bytes accessed | tf_op | source)
XLA Modules:
  0.0 61.4 jit_solution(1544619339986688031)
XLA Ops:
  0.6 2.0 %shard_map.68 = (s32[128,128]{1,0:T(8,128)}, s32[8,128]{1,0:T(8,128)S(1)}) custom-call(s32[8,128]{1,0:T(8,128)} %bitcast.22, s32[8,128]{1,0:T(8,128)} %bitcast.26), custom_call_target="tpu_custom_call" | custom-call | flops 1 | bytes 1 | tf_op jit(solution)/shard_map/pallas_call | solution.py:557
  2.7 11.5 %all-to-all-start = ((s32[128,1,128]{2,1,0:T(1,128)}), s32[128,1,128]{2,1,0:T(1,128)S(1)}, u32[]{:S(2)}, u32[]{:S(2)}) async-start(s32[128,1,128]{2,1,0:T(1,128)} %bitcast.3), calls=%async_computation | async-start | bytes 131072 | tf_op jit(solution)/shard_map/all_to_all | solution.py:497
  14.2 0.0 copy-start
  14.2 1.1 %copy-done = f32[6,4,32,256]{3,2,1,0:T(8,128)S(1)} copy-done((f32[6,4,32,256]{3,2,1,0:T(8,128)S(1)}, f32[6,4,32,256]{3,2,1,0:T(8,128)}, u32[]{:S(2)}) %copy-start) | copy-done | bytes 786456
  15.3 0.0 copy-start.1
  15.3 0.0 copy-start.2
  15.3 0.0 copy-start.3
  15.3 0.3 shard_map.69
  15.6 1.1 %collective-permute-start = (f32[6,4,8,256]{3,2,1,0:T(8,128)S(1)}, f32[6,4,8,256]{3,2,1,0:T(8,128)S(1)}, u32[]{:S(2)}, u32[]{:S(2)}) collective-permute-start(f32[6,4,8,256]{3,2,1,0:T(8,128)S(1)} %get-tuple-element.28), channel_id=1, source_target_pairs={{0,1},{1,0},{2,3},{3,2},{4,5},{5,4},{6,7},{7,6},{8,9},{9,8},{10,11... | collective-permute-start | bytes 589832 | tf_op jit(solution)/shard_map/ppermute | solution.py:581
  16.8 0.8 %collective-permute-start.1 = (f32[6,32,256]{2,1,0:T(8,128)S(1)}, f32[6,32,256]{2,1,0:T(8,128)S(1)}, u32[]{:S(2)}, u32[]{:S(2)}) collective-permute-start(f32[6,32,256]{2,1,0:T(8,128)S(1)} %get-tuple-element.29), channel_id=1, source_target_pairs={{0,2},{2,4},{4,6},{6,8},{8,10},{10,12},{12,14},{14,16},{16,18},{18... | collective-permute-start | bytes 589832 | tf_op jit(solution)/shard_map/ppermute | solution.py:582
  17.6 6.2 %collective-permute-start.2 = (f32[6,32,256]{2,1,0:T(8,128)S(1)}, f32[6,32,256]{2,1,0:T(8,128)S(1)}, u32[]{:S(2)}, u32[]{:S(2)}) collective-permute-start(f32[6,32,256]{2,1,0:T(8,128)S(1)} %get-tuple-element.30), channel_id=1, source_target_pairs={{2,0},{4,2},{6,4},{8,6},{10,8},{12,10},{14,12},{16,14},{18,16},{20... | collective-permute-start | bytes 589832 | tf_op jit(solution)/shard_map/ppermute | solution.py:583
  23.8 0.0 all-to-all-done
  23.8 2.5 %shard_map.70 = f32[128,128]{1,0:T(8,128)} custom-call(s32[128,128]{1,0:T(8,128)S(1)} %bitcast.18, bf16[640,512]{1,0:T(8,128)(2,1)S(1)} %get-tuple-element.27.table_ref), custom_call_target="tpu_custom_call" | custom-call | flops 1000000000 | bytes 1 | tf_op jit(solution)/shard_map/pallas_call | solution.py:584
  26.3 4.3 %all-to-all-start.1 = ((f32[128,1,128]{2,1,0:T(1,128)}), f32[128,1,128]{2,1,0:T(1,128)S(1)}, u32[]{:S(2)}, u32[]{:S(2)}) async-start(f32[128,1,128]{2,1,0:T(1,128)} %bitcast.6), calls=%async_computation.1 | async-start | bytes 131072 | tf_op jit(solution)/shard_map/all_to_all | solution.py:497
  30.6 0.0 collective-permute-done.edge_ref
  30.6 0.0 collective-permute-done.1.below
  30.6 0.0 collective-permute-done.2.above
  30.7 0.0 copy-done.1
  30.7 0.1 shard_map.71
  30.8 1.7 %collective-permute-start.3 = (f32[6,72,256]{2,1,0:T(8,128)S(1)}, f32[6,72,256]{2,1,0:T(8,128)S(1)}, u32[]{:S(2)}, u32[]{:S(2)}) collective-permute-start(f32[6,72,256]{2,1,0:T(8,128)S(1)} %get-tuple-element.41), channel_id=1, source_target_pairs={{0,2},{2,4},{4,6},{6,8},{8,10},{10,12},{12,14},{14,16},{16,18},{18... | collective-permute-start | bytes 1327112 | tf_op jit(solution)/shard_map/ppermute | solution.py:594
  32.4 6.3 %collective-permute-start.4 = (f32[6,72,256]{2,1,0:T(8,128)S(1)}, f32[6,72,256]{2,1,0:T(8,128)S(1)}, u32[]{:S(2)}, u32[]{:S(2)}) collective-permute-start(f32[6,72,256]{2,1,0:T(8,128)S(1)} %get-tuple-element.42), channel_id=1, source_target_pairs={{2,0},{4,2},{6,4},{8,6},{10,8},{12,10},{14,12},{16,14},{18,16},{20... | collective-permute-start | bytes 1327112 | tf_op jit(solution)/shard_map/ppermute | solution.py:595
  38.7 0.0 copy-done.2
  38.7 0.0 copy-done.3
  38.7 0.5 shard_map.72
  39.2 0.8 %all-to-all-done.1 = f32[128,1,128]{2,1,0:T(1,128)S(1)} async-done(((f32[128,1,128]{2,1,0:T(1,128)}), f32[128,1,128]{2,1,0:T(1,128)S(1)}, u32[]{:S(2)}, u32[]{:S(2)}) %all-to-all-start.1) | async-done | bytes 65568 | tf_op jit(solution)/shard_map/all_to_all | solution.py:497
  40.0 4.8 %shard_map.73 = (f32[5,1024,128]{2,1,0:T(8,128)}, f32[128,128]{1,0:T(8,128)}) custom-call(f32[128,128]{1,0:T(8,128)S(1)} %bitcast.21, bf16[1024,128]{1,0:T(8,128)(2,1)S(1)} %get-tuple-element.35.hot_ref, bf16[128,1024]{1,0:T(8,128)(2,1)S(1)} %get-tuple-element.36.turned_ref, bf16[1024,128]{1,0:T(8,128)(2,1)S(1)} %get-tuple-element.37.code_ref, ...), custom_call_target="tpu_custom_call" | custom-call | flops 10000000000 | bytes 5242880 | tf_op jit(solution)/shard_map/pallas_call | solution.py:525
  44.9 4.6 %all-to-all-start.2 = ((f32[128,1,128]{2,1,0:T(1,128)}), f32[128,1,128]{2,1,0:T(1,128)S(1)}, u32[]{:S(2)}, u32[]{:S(2)}) async-start(f32[128,1,128]{2,1,0:T(1,128)} %bitcast.10), calls=%async_computation.2 | async-start | bytes 131072 | tf_op jit(solution)/shard_map/all_to_all | solution.py:497
  49.5 0.0 collective-permute-done.3.low
  49.5 0.0 collective-permute-done.4.high
  49.5 8.0 %shard_map.74 = f32[6,4,32,256]{3,2,1,0:T(8,128)S(1)} custom-call(f32[6,4,32,256]{3,2,1,0:T(8,128)} %gas_ref.4, f32[6,4,8,256]{3,2,1,0:T(8,128)S(1)} %collective-permute-done.edge_ref, f32[6,32,256]{2,1,0:T(8,128)S(1)} %collective-permute-done.1.below, f32[6,32,256]{2,1,0:T(8,128)S(1)} %collective-permute-done.2.above, ...), custom_call_target="tpu_custom_call" | custom-call | flops 1 | bytes 1 | tf_op jit(solution)/shard_map/pallas_call | solution.py:603
  57.5 1.5 %all-to-all-done.2 = f32[128,1,128]{2,1,0:T(1,128)S(1)} async-done(((f32[128,1,128]{2,1,0:T(1,128)}), f32[128,1,128]{2,1,0:T(1,128)S(1)}, u32[]{:S(2)}, u32[]{:S(2)}) %all-to-all-start.2) | async-done | bytes 65568 | tf_op jit(solution)/shard_map/all_to_all | solution.py:497
  59.0 2.5 %shard_map.75 = f32[6,128,256]{2,1,0:T(8,128)} custom-call(s32[128,128]{1,0:T(8,128)S(1)} %bitcast.19, f32[128,128]{1,0:T(8,128)S(1)} %bitcast.20, f32[6,128,256]{2,1,0:T(8,128)S(1)} %bitcast.17), custom_call_target="tpu_custom_call" | custom-call | flops 1 | bytes 1 | tf_op jit(solution)/shard_map/pallas_call | solution.py:616
Async XLA Ops:
  2.7 21.1 %all-to-all-start = ((s32[128,1,128]{2,1,0:T(1,128)}), s32[128,1,128]{2,1,0:T(1,128)S(1)}, u32[]{:S(2)}, u32[]{:S(2)}) async-start(s32[128,1,128]{2,1,0:T(1,128)} %bitcast.3), calls=%async_computation | async-start | bytes 131072 | tf_op jit(solution)/shard_map/all_to_all | solution.py:497
  14.2 1.1 %copy-start = (f32[6,4,32,256]{3,2,1,0:T(8,128)S(1)}, f32[6,4,32,256]{3,2,1,0:T(8,128)}, u32[]{:S(2)}) copy-start(f32[6,4,32,256]{3,2,1,0:T(8,128)} %gas_ref.4) | copy-start | bytes 2359300
  15.3 15.3 %copy-start.1 = (f32[6,4,32,256]{3,2,1,0:T(8,128)S(1)}, f32[6,4,32,256]{3,2,1,0:T(8,128)}, u32[]{:S(2)}) copy-start(f32[6,4,32,256]{3,2,1,0:T(8,128)} %gas_ref.4) | copy-start | bytes 2359300
  15.3 23.4 %copy-start.2 = (s32[1024,1]{0,1:T(1,128)S(1)}, s32[1024,1]{0,1:T(1,128)}, u32[]{:S(2)}) copy-start(s32[1024,1]{0,1:T(1,128)} %param.7) | copy-start | bytes 12292
  15.3 23.4 %copy-start.3 = (s32[1024]{0:T(1024)S(1)}, s32[1024]{0:T(1024)}, u32[]{:S(2)}) copy-start(s32[1024]{0:T(1024)} %param.9) | copy-start | bytes 12292
  15.6 15.0 %collective-permute-start = (f32[6,4,8,256]{3,2,1,0:T(8,128)S(1)}, f32[6,4,8,256]{3,2,1,0:T(8,128)S(1)}, u32[]{:S(2)}, u32[]{:S(2)}) collective-permute-start(f32[6,4,8,256]{3,2,1,0:T(8,128)S(1)} %get-tuple-element.28), channel_id=1, source_target_pairs={{0,1},{1,0},{2,3},{3,2},{4,5},{5,4},{6,7},{7,6},{8,9},{9,8},{10,11... | collective-permute-start | bytes 589832 | tf_op jit(solution)/shard_map/ppermute | solution.py:581
  16.8 13.9 %collective-permute-start.1 = (f32[6,32,256]{2,1,0:T(8,128)S(1)}, f32[6,32,256]{2,1,0:T(8,128)S(1)}, u32[]{:S(2)}, u32[]{:S(2)}) collective-permute-start(f32[6,32,256]{2,1,0:T(8,128)S(1)} %get-tuple-element.29), channel_id=1, source_target_pairs={{0,2},{2,4},{4,6},{6,8},{8,10},{10,12},{12,14},{14,16},{16,18},{18... | collective-permute-start | bytes 589832 | tf_op jit(solution)/shard_map/ppermute | solution.py:582
  17.6 13.1 %collective-permute-start.2 = (f32[6,32,256]{2,1,0:T(8,128)S(1)}, f32[6,32,256]{2,1,0:T(8,128)S(1)}, u32[]{:S(2)}, u32[]{:S(2)}) collective-permute-start(f32[6,32,256]{2,1,0:T(8,128)S(1)} %get-tuple-element.30), channel_id=1, source_target_pairs={{2,0},{4,2},{6,4},{8,6},{10,8},{12,10},{14,12},{16,14},{18,16},{20... | collective-permute-start | bytes 589832 | tf_op jit(solution)/shard_map/ppermute | solution.py:583
  26.3 13.8 %all-to-all-start.1 = ((f32[128,1,128]{2,1,0:T(1,128)}), f32[128,1,128]{2,1,0:T(1,128)S(1)}, u32[]{:S(2)}, u32[]{:S(2)}) async-start(f32[128,1,128]{2,1,0:T(1,128)} %bitcast.6), calls=%async_computation.1 | async-start | bytes 131072 | tf_op jit(solution)/shard_map/all_to_all | solution.py:497
  30.8 18.8 %collective-permute-start.3 = (f32[6,72,256]{2,1,0:T(8,128)S(1)}, f32[6,72,256]{2,1,0:T(8,128)S(1)}, u32[]{:S(2)}, u32[]{:S(2)}) collective-permute-start(f32[6,72,256]{2,1,0:T(8,128)S(1)} %get-tuple-element.41), channel_id=1, source_target_pairs={{0,2},{2,4},{4,6},{6,8},{8,10},{10,12},{12,14},{14,16},{16,18},{18... | collective-permute-start | bytes 1327112 | tf_op jit(solution)/shard_map/ppermute | solution.py:594
  32.4 17.1 %collective-permute-start.4 = (f32[6,72,256]{2,1,0:T(8,128)S(1)}, f32[6,72,256]{2,1,0:T(8,128)S(1)}, u32[]{:S(2)}, u32[]{:S(2)}) collective-permute-start(f32[6,72,256]{2,1,0:T(8,128)S(1)} %get-tuple-element.42), channel_id=1, source_target_pairs={{2,0},{4,2},{6,4},{8,6},{10,8},{12,10},{14,12},{16,14},{18,16},{20... | collective-permute-start | bytes 1327112 | tf_op jit(solution)/shard_map/ppermute | solution.py:595
  44.9 14.1 %all-to-all-start.2 = ((f32[128,1,128]{2,1,0:T(1,128)}), f32[128,1,128]{2,1,0:T(1,128)S(1)}, u32[]{:S(2)}, u32[]{:S(2)}) async-start(f32[128,1,128]{2,1,0:T(1,128)} %bitcast.10), calls=%async_computation.2 | async-start | bytes 131072 | tf_op jit(solution)/shard_map/all_to_all | solution.py:497
